TPU v7x, 32 devices: a whole 2x2x4 slice. The times are simulated.
32 devices in a mesh: node: 4 (over y, core), hst: 8 (over z, x).
Axes of the slice: x: 2, y: 2, z: 4, core: 2. Of those that a mesh axis runs over, the one named last changes fastest.
Arguments:
- hidden: bfloat16 [8, 4096, 640], P('hst', 'node'), may hold values from -6 to 6
- cotangent: bfloat16 [8, 4096, 4608], P('hst', 'node'), may hold values from -12 to 12
- anchor: float32 [8, 640, 4608], P('hst', 'node'), may hold values from -0.25 to 0.25
- momentum: float32 [8, 640, 4608], P('hst', 'node'), may hold values from -0.6 to 0.6
- round_mask: int32 [1], replicated, may hold values from 1 to 7
Outputs:
- weights_out: bfloat16 [8, 640, 4608], P('hst')
- momentum_out: float32 [8, 640, 4608], P('hst', 'node')
Inputs may be any that keep to these rules, and one draw needn't show every extreme that they name: round_mask is the same for all hosts; host i averages with the hosts i XOR s for every s whose bits lie within round_mask.
All inputs are finite; a program needn't handle non-finite values.
Results may differ from a plain program's by a relative error of at most 0.009.
Values may be sent and summed in bfloat16 or wider, within the bound.
No kernel may reach another device: no remote copies, remote signals or barrier semaphores. Data moves between devices by JAX's collectives and lax.ppermute only.
A program may use at most 256 MiB of HBM per device.

v0:
```python
import jax
import jax.numpy as jnp
from jax import lax
from jax.sharding import PartitionSpec as P

base_rate = 0.5
slow_rate = 1.0
slow_beta = 0.7


def swapped(block, axis, bit):
    count = lax.axis_size(axis)
    route = []
    for low in range(count):
        high = low | 1 << bit
        if high != low and high < count:
            route += [(low, high), (high, low)]
    return lax.ppermute(block, axis, route)


def half_step(current, bit_index):
    other_rows = swapped(current.astype(jnp.bfloat16), "hst", bit_index).astype(current.dtype)
    return 0.5 * (current + other_rows)


def local(hidden, cotangent, anchor, momentum, round_mask):
    tokens_here = hidden[0]
    grads_in = cotangent[0]
    token_scale = 1.0 / (tokens_here.shape[0] * lax.axis_size("node"))
    product = lax.dot_general(
        tokens_here, grads_in, (((0,), (0,)), ((), ())), preferred_element_type=jnp.float32
    )
    gradient = lax.psum_scatter(
        (product * token_scale).astype(jnp.bfloat16), "node", scatter_dimension=0, tiled=True
    ).astype(jnp.float32)
    stepped = anchor[0] - base_rate * gradient
    mask_value = round_mask[0]
    host_count = lax.axis_size("hst")
    bit_count = host_count.bit_length() - 1
    bit_list = list(range(bit_count))
    averaged = stepped
    for bit_index in bit_list:
        active = jnp.bitwise_and(jnp.right_shift(mask_value, bit_index), 1) == 1
        averaged = jnp.where(active, half_step(averaged, bit_index), averaged)
    momentum_new = slow_beta * momentum[0] + (anchor[0] - averaged) / base_rate
    updated = (anchor[0] - slow_rate * base_rate * momentum_new).astype(jnp.bfloat16)
    weights_whole = lax.all_gather(updated[None], "node", axis=1, tiled=True)
    return (weights_whole, momentum_new[None])


def solution(mesh):
    placed = (
        P("hst", "node", None),
        P("hst", "node", None),
        P("hst", "node", None),
        P("hst", "node", None),
        P(),
    )
    return jax.shard_map(
        local,
        mesh=mesh,
        in_specs=placed,
        out_specs=(P("hst", None, None), P("hst", "node", None)),
        check_vma=False,
    )
```

profile of v0, /device:TPU:0, one launch (start us, length us, event | category | flops | bytes accessed | tf_op | source)
XLA Modules:
  0.0 274.5 jit_solution(9448311714067848026)
XLA Ops:
  7.2 0.0 copy-start
  7.2 0.0 reduce-scatter.2.cloned.1.call-start
  7.2 1.3 copy-done
  8.5 10.5 %multiply_convert_fusion = bf16[640,4608]{1,0:T(8,128)(2,1)} fusion(bf16[1,1024,4608]{2,1,0:T(8,128)(2,1)} %param.6, bf16[1,1024,640]{2,1,0:T(8,128)(2,1)S(1)} %copy-done), kind=kOutput, calls=%fused_computation | convolution fusion | flops 6045696000 | bytes 16646144 | tf_op jit(solution)/shard_map/dot_general | solution.py:30
  19.0 0.0 reduce-scatter.2.cloned.1.call-update
  19.0 0.0 all-gather.3.cloned.1.call-start
  19.0 58.5 %reduce-scatter.2.cloned.1.call-done = bf16[160,4608]{1,0:T(8,128)(2,1)} async-done(((bf16[640,4608]{1,0:T(8,128)(2,1)}), bf16[160,4608]{1,0:T(8,128)(2,1)}) %reduce-scatter.2.cloned.1.call-update) | async-done | bytes 1474576 | tf_op jit(solution)/shard_map/reduce_scatter | solution.py:33
  77.6 0.0 copy-start.1
  77.6 0.0 copy-start.2
  77.6 2.8 %fusion.6 = bf16[160,4608]{1,0:T(8,128)(2,1)S(1)} fusion(bf16[160,4608]{1,0:T(8,128)(2,1)} %reduce-scatter.2.cloned.1.call-done, f32[1,160,4608]{2,1,0:T(8,128)} %param.7), kind=kLoop, calls=%fused_computation.11 | loop fusion | flops 2949120 | bytes 5898240 | tf_op jit(solution)/shard_map/convert_element_type | solution.py:22
  80.3 1.5 collective-permute-start
  82.5 31.9 %collective-permute-done = bf16[160,4608]{1,0:T(8,128)(2,1)S(1)} collective-permute-done((bf16[160,4608]{1,0:T(8,128)(2,1)S(1)}, bf16[160,4608]{1,0:T(8,128)(2,1)S(1)}, u32[]{:S(2)}, u32[]{:S(2)}) %collective-permute-start) | collective-permute-done | bytes 1474592 | tf_op jit(solution)/shard_map/ppermute | solution.py:18
  114.4 0.0 copy-done.1
  114.4 0.0 copy-done.2
  114.4 0.7 fusion.9
  115.2 1.5 collective-permute-start.1
  116.7 31.7 %collective-permute-done.1 = bf16[160,4608]{1,0:T(8,128)(2,1)S(1)} collective-permute-done((bf16[160,4608]{1,0:T(8,128)(2,1)S(1)}, bf16[160,4608]{1,0:T(8,128)(2,1)S(1)}, u32[]{:S(2)}, u32[]{:S(2)}) %collective-permute-start.1) | collective-permute-done | bytes 1474592 | tf_op jit(solution)/shard_map/ppermute | solution.py:18
  148.4 0.0 copy-start.3
  148.4 1.1 fusion.7
  149.5 2.5 collective-permute-start.2
  152.0 62.3 %collective-permute-done.2 = bf16[160,4608]{1,0:T(8,128)(2,1)S(1)} collective-permute-done((bf16[160,4608]{1,0:T(8,128)(2,1)S(1)}, bf16[160,4608]{1,0:T(8,128)(2,1)S(1)}, u32[]{:S(2)}, u32[]{:S(2)}) %collective-permute-start.2) | collective-permute-done | bytes 1474592 | tf_op jit(solution)/shard_map/ppermute | solution.py:18
  214.3 0.0 copy-done.3
  214.3 3.5 %fusion.5 = (bf16[160,4608]{1,0:T(8,128)(2,1)}, f32[160,4608]{1,0:T(8,128)}) fusion(f32[1,160,4608]{2,1,0:T(8,128)S(1)} %copy-done.1, bf16[160,4608]{1,0:T(8,128)(2,1)S(1)} %collective-permute-done.2, bf16[160,4608]{1,0:T(8,128)(2,1)S(1)} %collective-permute-done.1, bf16[160,4608]{1,0:T(8,128)(2,1)S(1)} %collective-permute-done, ...), kind=kLoop, calls=%fused_computation.8 | loop fusion | flops 16220160 | bytes 16220163 | tf_op jit(solution)/shard_map/convert_element_type | solution.py:46
  217.7 0.0 all-gather.3.cloned.1.call-update
  217.8 44.3 %all-gather.3.cloned.1.call-done = bf16[640,4608]{1,0:T(8,128)(2,1)} async-done(((bf16[160,4608]{1,0:T(8,128)(2,1)}), bf16[640,4608]{1,0:T(8,128)(2,1)}) %all-gather.3.cloned.1.call-update) | async-done | bytes 5898256 | tf_op jit(solution)/shard_map/all_gather | solution.py:47
  262.1 5.6 %copy.9 = bf16[1,640,4608]{2,1,0:T(8,128)(2,1)} copy(bf16[1,640,4608]{2,1,0:T(8,128)(2,1)} %bitcast.37) | data formatting | bytes 11796480
Async XLA Ops:
  7.2 1.3 copy-start
  7.2 70.4 %reduce-scatter.2.cloned.1.call-start = ((), (), s32[]{:S(2)}) async-start(), calls=%async_computation.1 | async-start | bytes 7372800 | tf_op jit(solution)/shard_map/reduce_scatter | solution.py:33
  19.0 243.1 %all-gather.3.cloned.1.call-start = ((), (), s32[]{:S(2)}) async-start(), calls=%async_computation.2 | async-start | bytes 7372800 | tf_op jit(solution)/shard_map/all_gather | solution.py:47
  77.6 36.9 %copy-start.1 = (f32[1,160,4608]{2,1,0:T(8,128)S(1)}, f32[1,160,4608]{2,1,0:T(8,128)}, u32[]{:S(2)}) copy-start(f32[1,160,4608]{2,1,0:T(8,128)} %param.7) | copy-start | bytes 8847364
  77.6 36.9 %copy-start.2 = (bf16[160,4608]{1,0:T(8,128)(2,1)S(1)}, bf16[160,4608]{1,0:T(8,128)(2,1)}, u32[]{:S(2)}) copy-start(bf16[160,4608]{1,0:T(8,128)(2,1)} %reduce-scatter.2.cloned.1.call-done) | copy-start | bytes 4423684
  80.3 34.1 %collective-permute-start = (bf16[160,4608]{1,0:T(8,128)(2,1)S(1)}, bf16[160,4608]{1,0:T(8,128)(2,1)S(1)}, u32[]{:S(2)}, u32[]{:S(2)}) collective-permute-start(bf16[160,4608]{1,0:T(8,128)(2,1)S(1)} %fusion.6), channel_id=1, source_target_pairs={{0,1},{1,0},{2,3},{3,2},{4,5},{5,4},{6,7},{7,6},{8,9},{9,8},{10,11... | collective-permute-start | bytes 4423688 | tf_op jit(solution)/shard_map/ppermute | solution.py:18
  115.2 33.2 %collective-permute-start.1 = (bf16[160,4608]{1,0:T(8,128)(2,1)S(1)}, bf16[160,4608]{1,0:T(8,128)(2,1)S(1)}, u32[]{:S(2)}, u32[]{:S(2)}) collective-permute-start(bf16[160,4608]{1,0:T(8,128)(2,1)S(1)} %fusion.9), channel_id=1, source_target_pairs={{0,2},{2,0},{1,3},{3,1},{4,6},{6,4},{5,7},{7,5},{8,10},{10,8},{9,1... | collective-permute-start | bytes 4423688 | tf_op jit(solution)/shard_map/ppermute | solution.py:18
  148.4 65.9 %copy-start.3 = (f32[1,160,4608]{2,1,0:T(8,128)S(1)}, f32[1,160,4608]{2,1,0:T(8,128)}, u32[]{:S(2)}) copy-start(f32[1,160,4608]{2,1,0:T(8,128)} %param.8) | copy-start | bytes 8847364
  149.5 64.8 %collective-permute-start.2 = (bf16[160,4608]{1,0:T(8,128)(2,1)S(1)}, bf16[160,4608]{1,0:T(8,128)(2,1)S(1)}, u32[]{:S(2)}, u32[]{:S(2)}) collective-permute-start(bf16[160,4608]{1,0:T(8,128)(2,1)S(1)} %fusion.7), channel_id=1, source_target_pairs={{0,4},{4,0},{1,5},{5,1},{2,6},{6,2},{3,7},{7,3},{8,12},{12,8},{9,1... | collective-permute-start | bytes 4423688 | tf_op jit(solution)/shard_map/ppermute | solution.py:18
Sparse Core Ops, SparseCore 0:
  19.1 58.4 reduce-scatter.1
  217.9 44.1 all-gather.2
where the time goes:
time: 275 us
  waiting for transfers between devices  229 us (83%)
  between operations  14.7 us (5%)
  matrix products  10.5 us (4%)
  other arithmetic  8.04 us (3%)
  local copies, waits for them, and re-layouts  6.9 us (3%)
  starting transfers between devices  5.65 us (2%)
    ppermute x3, waiting for transfers between devices, swapped(): return lax.ppermute(block, axis, route)  126 us
    reduce_scatter x1, waiting for transfers between devices, local(): lax.psum_scatter((product * token_scale).astype(jnp.bfloat16), 'node', sc...  58.5 us
    all_gather x1, waiting for transfers between devices, local(): weights_whole = lax.all_gather(updated[None], 'node', axis=1, tiled=True)  44.3 us
    dot_general x1, matrix products, local(): lax.dot_general(tokens_here, grads_in, (((0,), (0,)), ((), ())), preferre...  10.5 us
    unnamed x9, local copies, waits for them, and re-layouts  6.9 us
    ppermute x3, starting transfers between devices, swapped(): return lax.ppermute(block, axis, route)  5.57 us
  transfers between devices with their start and end apart: 5, of which 5 were waited for; matrix products, arithmetic and copies ran while one was open for 0% of the time, Pallas kernels for 0%

commit v1 on v0

v1 whole, which is shorter than its diff:
```python
import jax
import jax.numpy as jnp
from jax import lax
from jax.sharding import PartitionSpec as P

base_rate = 0.5
slow_rate = 1.0
slow_beta = 0.7
chunk_count = 2


def swapped(block, axis, bit):
    count = lax.axis_size(axis)
    return lax.ppermute(block, axis, [(i, i ^ (1 << bit)) for i in range(count)])


def pick(flag, pair):
    return jnp.where(flag == 1, pair[1], pair[0])


def half_of(index, bit):
    return jnp.bitwise_and(jnp.right_shift(index, bit), 1)


def node_sum(parts, node, bits):
    for bit in bits:
        mine = half_of(node, bit)
        low, high = parts[0::2], parts[1::2]
        send = [jnp.where(mine == 1, a, b).astype(jnp.bfloat16) for a, b in zip(low, high)]
        keep = [jnp.where(mine == 1, b, a) for a, b in zip(low, high)]
        got = swapped(jnp.stack(send), "node", bit)
        parts = [k + g.astype(jnp.float32) for k, g in zip(keep, got)]
    return parts[0]


def host_mean(block, host, order):
    halved = []
    count = 1
    rows = block.shape[0]
    for place, bit in enumerate(order):
        count *= 2
        if place < len(order) - 1 and rows % 16 == 0 and len(halved) < 2:
            rows //= 2
            mine = half_of(host, bit)
            low, high = block[:rows], block[rows:]
            got = swapped(pick(mine, (high, low)).astype(jnp.bfloat16), "hst", bit)
            block = pick(mine, (low, high)) + got.astype(jnp.float32)
            halved.append(bit)
        else:
            block = block + swapped(block.astype(jnp.bfloat16), "hst", bit).astype(jnp.float32)
    block = block * (1.0 / count)
    for bit in reversed(halved):
        mine = half_of(host, bit)
        got = swapped(block.astype(jnp.bfloat16), "hst", bit).astype(jnp.float32)
        block = jnp.concatenate([pick(mine, (block, got)), pick(mine, (got, block))], axis=0)
    return block


def update(orders, hidden, cotangent, anchor, momentum):
    tokens, width = cotangent.shape
    node_count = lax.axis_size("node")
    node_bits = range(node_count.bit_length() - 1)
    node, host = lax.axis_index("node"), lax.axis_index("hst")
    rows = anchor.shape[0]
    scale = 1.0 / (tokens * node_count)
    part = width // chunk_count
    weights = jnp.zeros((rows * node_count, width), jnp.bfloat16)
    momentum_parts = []
    for chunk in range(chunk_count):
        columns = slice(chunk * part, (chunk + 1) * part)
        product = lax.dot_general(
            hidden, cotangent[:, columns], (((0,), (0,)), ((), ())), preferred_element_type=jnp.float32
        ) * scale
        gradient = node_sum(list(product.reshape(node_count, rows, part)), node, node_bits)
        stepped = anchor[:, columns] - base_rate * gradient
        averaged = host_mean(stepped, host, orders[chunk % len(orders)])
        momentum_new = slow_beta * momentum[:, columns] + (anchor[:, columns] - averaged) / base_rate
        momentum_parts.append(momentum_new)
        updated = (anchor[:, columns] - slow_rate * base_rate * momentum_new).astype(jnp.bfloat16)
        have = [(node, updated)]
        for bit in reversed(node_bits):
            have += [(place ^ (1 << bit), swapped(block, "node", bit)) for place, block in have]
        for place, block in have:
            weights = lax.dynamic_update_slice(weights, block, (place * rows, chunk * part))
    return weights, jnp.concatenate(momentum_parts, axis=1)


def local(hidden, cotangent, anchor, momentum, round_mask):
    host_count = lax.axis_size("hst")
    branches = []
    for mask in range(1, host_count):
        bits = [b for b in range(host_count.bit_length() - 1) if mask >> b & 1]
        orders = [bits, bits[:-1][::-1] + bits[-1:]]
        branches.append(lambda *arrays, orders=orders: update(orders, *arrays))
    weights, momentum_new = lax.switch(
        round_mask[0] - 1, branches, hidden[0], cotangent[0], anchor[0], momentum[0]
    )
    return (weights[None], momentum_new[None])


def solution(mesh):
    placed = (
        P("hst", "node", None),
        P("hst", "node", None),
        P("hst", "node", None),
        P("hst", "node", None),
        P(),
    )
    return jax.shard_map(
        local,
        mesh=mesh,
        in_specs=placed,
        out_specs=(P("hst", None, None), P("hst", "node", None)),
        check_vma=False,
    )
```

time: 275 us -> 202 us (0.73)
  waiting for transfers between devices: 229 us -> 92.6 us
  loops' own time: 0 us -> 34.6 us
  other arithmetic: 8.04 us -> 23.8 us
  starting transfers between devices: 5.65 us -> 20.3 us
  between operations: 14.7 us -> 2.42 us
  local copies, waits for them, and re-layouts: 6.9 us -> 16.2 us
    reduce_scatter x1 -> x0, waiting for transfers between devices: 58.5 us -> none  [local(): lax.psum_scatter((product * token_scale).astype(jnp.bfloat16), 'node', sc...]
    all_gather x1 -> x0, waiting for transfers between devices: 44.3 us -> none  [local(): weights_whole = lax.all_gather(updated[None], 'node', axis=1, tiled=True)]
    another operation x0 -> x1, loops' own time: none -> 34.6 us  [local(): lax.switch(round_mask[0] - 1, branches, hidden[0], cotangent[0], anchor[0...]
    ppermute x3 -> x20, waiting for transfers between devices: 126 us -> 92.6 us  [swapped(): return lax.ppermute(block, axis, [(i, i ^ 1 << bit) for i in range(count)])]
    ppermute x3 -> x20, starting transfers between devices: 5.57 us -> 20.3 us  [swapped(): return lax.ppermute(block, axis, [(i, i ^ 1 << bit) for i in range(count)])]
    another operation x0 -> x6, other arithmetic: none -> 9.28 us  [node_sum(): got = swapped(jnp.stack(send), 'node', bit)]
    cond x0 -> x24, local copies, waits for them, and re-layouts: none -> 9.27 us
    unnamed x9 -> x0, local copies, waits for them, and re-layouts: 6.9 us -> none
  transfers between devices with their start and end apart: 5 -> 20, of which waited for: 5 -> 12; matrix products, arithmetic and copies ran while one was open for 0% -> 12% of each run, Pallas kernels for 0% -> 0%
where the time goes in v1:
time: 202 us; the launch traced here: 199 us
  waiting for transfers between devices  92.6 us (46%)
  loops' own time  34.6 us (17%)
  other arithmetic  23.8 us (12%)
  starting transfers between devices  20.3 us (10%)
  local copies, waits for them, and re-layouts  16.2 us (8%)
  matrix products  9.4 us (5%)
  between operations  2.42 us (1%)
    ppermute x20, waiting for transfers between devices, swapped(): return lax.ppermute(block, axis, [(i, i ^ 1 << bit) for i in range(count)])  92.6 us
    another operation x1, loops' own time, local(): lax.switch(round_mask[0] - 1, branches, hidden[0], cotangent[0], anchor[0...  34.6 us
    ppermute x20, starting transfers between devices, swapped(): return lax.ppermute(block, axis, [(i, i ^ 1 << bit) for i in range(count)])  20.3 us
    dot_general x2, matrix products, update(): lax.dot_general(hidden, cotangent[:, columns], (((0,), (0,)), ((), ())),...  9.4 us
    another operation x6, other arithmetic, node_sum(): got = swapped(jnp.stack(send), 'node', bit)  9.28 us
    cond x24, local copies, waits for them, and re-layouts  9.27 us
    sub x1, other arithmetic, update(): stepped = anchor[:, columns] - base_rate * gradient  6.61 us
    dynamic_update_slice x6, local copies, waits for them, and re-layouts, update(): lax.dynamic_update_slice(weights, block, (place * rows, chunk * part))  6.58 us
  transfers between devices with their start and end apart: 20, of which 12 were waited for; matrix products, arithmetic and copies ran while one was open for 12% of the time, Pallas kernels for 0%

profile of v1, /device:TPU:0, one launch (start us, length us, event | category | flops | bytes accessed | tf_op | source)
XLA Modules:
  0.0 199.4 jit_solution(5578485841259934463)
XLA Ops:
  1.3 197.0 %conditional.1 = (bf16[1,640,4608]{2,1,0:T(8,128)(2,1)}, f32[1,160,4608]{2,1,0:T(8,128)}) conditional(s32[]{:T(128)} %bitcast.147, (f32[160,4608]{1,0:T(8,128)}, f32[160,4608]{1,0:T(8,128)}, bf16[1024,4608]{1,0:T(8,128)(2,1)}, bf16[1024,640]{1,0:T(8,128)(2,1)}) %tuple.168, (f32[160,4608]{1,0:T(8,128)}, ...), branch_computations={%region_0.1_spmd, %region_1.2_spmd, %region_2.3_spmd, %region_3.4_... | conditional | flops 6073528320 | bytes 382403584 | solution.py:95
  35.4 6.1 %convolution_multiply_fusion.13 = f32[640,2304]{1,0:T(8,128)S(1)} fusion(bf16[1024,640]{1,0:T(8,128)(2,1)} %get-tuple-element.84, bf16[1024,4608]{1,0:T(8,128)(2,1)} %get-tuple-element.85), kind=kOutput, calls=%fused_computation.319 | convolution fusion | flops 3021373440 | bytes 11927552 | tf_op jit(solution)/shard_map/cond/branch_6_fun/dot_general | solution.py:71
  42.5 1.6 copy-done.83
  44.1 3.3 %convolution_multiply_fusion.12 = f32[640,2304]{1,0:T(8,128)S(1)} fusion(bf16[1024,640]{1,0:T(8,128)(2,1)S(1)} %copy-done.83, bf16[1024,4608]{1,0:T(8,128)(2,1)S(1)} %copy-done.76), kind=kOutput, calls=%fused_computation.318 | convolution fusion | flops 3021373440 | bytes 11927552 | tf_op jit(solution)/shard_map/cond/branch_6_fun/dot_general | solution.py:71
  47.7 2.3 %copy-done.28 = f32[640,2304]{1,0:T(8,128)} copy-done((f32[640,2304]{1,0:T(8,128)}, f32[640,2304]{1,0:T(8,128)S(1)}, u32[]{:S(2)}) %copy-start.28) | copy-done | bytes 5898264 | tf_op jit(solution)/shard_map/cond
  51.7 4.6 %fusion.102 = bf16[1,160,2304]{2,1,0:T(8,128)(2,1)} fusion(pred[]{:T(512)S(6)} %eq.60, bf16[2,160,2304]{2,1,0:T(8,128)(2,1)S(1)} %collective-permute-done.84, f32[640,2304]{1,0:T(8,128)} %copy-done.27, pred[]{:T(512)S(6)} %eq.61), kind=kLoop, calls=%fused_computation.355 | loop fusion | flops 2949120 | bytes 8110082 | tf_op jit(solution)/shard_map/cond/branch_6_fun/stack | solution.py:31
  56.3 2.5 %collective-permute-start.85 = (bf16[1,160,2304]{2,1,0:T(8,128)(2,1)}, bf16[1,160,2304]{2,1,0:T(8,128)(2,1)}, u32[]{:S(2)}, u32[]{:S(2)}) collective-permute-start(bf16[1,160,2304]{2,1,0:T(8,128)(2,1)} %fusion.102), channel_id=1, source_target_pairs={{0,16},{8,24},{16,0},{24,8},{1,17},{9,25},{17,1},{25,9},{2,18},{10... | collective-permute-start | bytes 2211848 | tf_op jit(solution)/shard_map/cond/branch_6_fun/ppermute | solution.py:14
  58.8 2.8 %fusion.105 = bf16[1,160,2304]{2,1,0:T(8,128)(2,1)} fusion(pred[]{:T(512)S(6)} %eq.60, bf16[2,160,2304]{2,1,0:T(8,128)(2,1)} %collective-permute-done.94, f32[640,2304]{1,0:T(8,128)S(1)} %copy-done.29, pred[]{:T(512)S(6)} %eq.61), kind=kLoop, calls=%fused_computation.358 | loop fusion | flops 2949120 | bytes 8110082 | tf_op jit(solution)/shard_map/cond/branch_6_fun/stack | solution.py:31
  62.2 14.2 %collective-permute-done.85 = bf16[1,160,2304]{2,1,0:T(8,128)(2,1)} collective-permute-done((bf16[1,160,2304]{2,1,0:T(8,128)(2,1)}, bf16[1,160,2304]{2,1,0:T(8,128)(2,1)}, u32[]{:S(2)}, u32[]{:S(2)}) %collective-permute-start.85) | collective-permute-done | bytes 737312 | tf_op jit(solution)/shard_map/cond/branch_6_fun/ppermute | solution.py:14
  76.5 15.6 %collective-permute-done.95 = bf16[1,160,2304]{2,1,0:T(8,128)(2,1)} collective-permute-done((bf16[1,160,2304]{2,1,0:T(8,128)(2,1)}, bf16[1,160,2304]{2,1,0:T(8,128)(2,1)}, u32[]{:S(2)}, u32[]{:S(2)}) %collective-permute-start.95) | collective-permute-done | bytes 737312 | tf_op jit(solution)/shard_map/cond/branch_6_fun/ppermute | solution.py:14
  92.1 6.6 %fusion.97 = (f32[160,2304]{1,0:T(8,128)S(1)}, f32[160,2304]{1,0:T(8,128)S(1)}) fusion(f32[160,4608]{1,0:T(8,128)S(1)} %copy-done.6, bf16[1,160,2304]{2,1,0:T(8,128)(2,1)} %collective-permute-done.95, pred[]{:T(512)S(6)} %eq.60, bf16[2,160,2304]{2,1,0:T(8,128)(2,1)} %collective-permute-done.94, f32[640,2304]{1,0:T(8,128)} %copy-done.28, pred[]{:T(512)S(6)} %eq.61, ...), kind=kLoop, calls=%fused_computation.333 | loop fusion | flops 8110080 | bytes 22118402 | tf_op jit(solution)/shard_map/cond/branch_6_fun/sub | solution.py:75
  98.8 1.8 collective-permute-start.86
  100.6 1.6 collective-permute-start.96
  102.3 7.0 %collective-permute-done.86 = bf16[80,2304]{1,0:T(8,128)(2,1)S(1)} collective-permute-done((bf16[80,2304]{1,0:T(8,128)(2,1)S(1)}, bf16[80,2304]{1,0:T(8,128)(2,1)S(1)}, u32[]{:S(2)}, u32[]{:S(2)}) %collective-permute-start.86) | collective-permute-done | bytes 368672 | tf_op jit(solution)/shard_map/cond/branch_6_fun/ppermute | solution.py:14
  109.4 1.7 collective-permute-start.87
  111.2 1.6 collective-permute-start.97
  112.8 2.3 %collective-permute-done.87 = bf16[40,2304]{1,0:T(8,128)(2,1)S(1)} collective-permute-done((bf16[40,2304]{1,0:T(8,128)(2,1)S(1)}, bf16[40,2304]{1,0:T(8,128)(2,1)S(1)}, u32[]{:S(2)}, u32[]{:S(2)}) %collective-permute-start.87) | collective-permute-done | bytes 184352 | tf_op jit(solution)/shard_map/cond/branch_6_fun/ppermute | solution.py:14
  115.2 2.6 %collective-permute-start.88 = (bf16[40,2304]{1,0:T(8,128)(2,1)S(1)}, bf16[40,2304]{1,0:T(8,128)(2,1)S(1)}, u32[]{:S(2)}, u32[]{:S(2)}) collective-permute-start(bf16[40,2304]{1,0:T(8,128)(2,1)S(1)} %get-tuple-element.158), channel_id=1, source_target_pairs={{0,4},{1,5},{2,6},{3,7},{4,0},{5,1},{6,2},{7,3},{8,12},{9,13},{10,... | collective-permute-start | bytes 552968 | tf_op jit(solution)/shard_map/cond/branch_6_fun/ppermute | solution.py:14
  117.8 1.7 collective-permute-start.98
  119.6 10.1 %collective-permute-done.88 = bf16[40,2304]{1,0:T(8,128)(2,1)S(1)} collective-permute-done((bf16[40,2304]{1,0:T(8,128)(2,1)S(1)}, bf16[40,2304]{1,0:T(8,128)(2,1)S(1)}, u32[]{:S(2)}, u32[]{:S(2)}) %collective-permute-start.88) | collective-permute-done | bytes 184352 | tf_op jit(solution)/shard_map/cond/branch_6_fun/ppermute | solution.py:14
  129.8 3.0 %collective-permute-done.98 = bf16[40,2304]{1,0:T(8,128)(2,1)S(1)} collective-permute-done((bf16[40,2304]{1,0:T(8,128)(2,1)S(1)}, bf16[40,2304]{1,0:T(8,128)(2,1)S(1)}, u32[]{:S(2)}, u32[]{:S(2)}) %collective-permute-start.98) | collective-permute-done | bytes 184352 | tf_op jit(solution)/shard_map/cond/branch_6_fun/ppermute | solution.py:14
  133.9 2.8 %collective-permute-done.89 = bf16[40,2304]{1,0:T(8,128)(2,1)S(1)} collective-permute-done((bf16[40,2304]{1,0:T(8,128)(2,1)S(1)}, bf16[40,2304]{1,0:T(8,128)(2,1)S(1)}, u32[]{:S(2)}, u32[]{:S(2)}) %collective-permute-start.89) | collective-permute-done | bytes 184352 | tf_op jit(solution)/shard_map/cond/branch_6_fun/ppermute | solution.py:14
  140.2 1.9 collective-permute-start.100
  142.1 4.6 %collective-permute-done.90 = bf16[80,2304]{1,0:T(8,128)(2,1)S(1)} collective-permute-done((bf16[80,2304]{1,0:T(8,128)(2,1)S(1)}, bf16[80,2304]{1,0:T(8,128)(2,1)S(1)}, u32[]{:S(2)}, u32[]{:S(2)}) %collective-permute-start.90) | collective-permute-done | bytes 368672 | tf_op jit(solution)/shard_map/cond/branch_6_fun/ppermute | solution.py:14
  147.2 1.4 copy-done.16
  148.7 1.8 bitcast_dynamic-update-slice_fusion.55
  150.5 2.6 %copy-done.48 = bf16[1,640,4608]{2,1,0:T(8,128)(2,1)} copy-done((bf16[1,640,4608]{2,1,0:T(8,128)(2,1)}, bf16[1,640,4608]{2,1,0:T(8,128)(2,1)S(1)}, u32[]{:S(2)}) %copy-start.48) | copy-done | bytes 5898264 | tf_op jit(solution)/shard_map/cond
  154.9 15.5 %collective-permute-done.91 = bf16[160,2304]{1,0:T(8,128)(2,1)} collective-permute-done((bf16[160,2304]{1,0:T(8,128)(2,1)}, bf16[160,2304]{1,0:T(8,128)(2,1)}, u32[]{:S(2)}, u32[]{:S(2)}) %collective-permute-start.91) | collective-permute-done | bytes 737312 | tf_op jit(solution)/shard_map/cond/branch_6_fun/ppermute | solution.py:14
  170.3 2.0 %bitcast_dynamic-update-slice_fusion.54 = bf16[1,640,4608]{2,1,0:T(8,128)(2,1)} fusion(bf16[1,640,4608]{2,1,0:T(8,128)(2,1)} %copy-done.48, s32[]{:T(128)S(6)} %select_n.637, bf16[160,2304]{1,0:T(8,128)(2,1)} %collective-permute-done.91), kind=kLoop, calls=%fused_computation.371 | loop fusion | bytes 1474564 | tf_op jit(solution)/shard_map/cond/branch_6_fun/dynamic_update_slice | solution.py:84
  174.7 1.2 bitcast_dynamic-update-slice_fusion.51
  176.5 1.9 maximum_bitcast_fusion.6
  178.4 16.4 %collective-permute-done.101 = bf16[160,2304]{1,0:T(8,128)(2,1)S(1)} collective-permute-done((bf16[160,2304]{1,0:T(8,128)(2,1)S(1)}, bf16[160,2304]{1,0:T(8,128)(2,1)S(1)}, u32[]{:S(2)}, u32[]{:S(2)}) %collective-permute-start.101) | collective-permute-done | bytes 737312 | tf_op jit(solution)/shard_map/cond/branch_6_fun/ppermute | solution.py:14
  (68 shorter events, 17.2 us)
Async XLA Ops:
  35.4 7.1 %copy-start.76 = (bf16[1024,4608]{1,0:T(8,128)(2,1)S(1)}, bf16[1024,4608]{1,0:T(8,128)(2,1)}, u32[]{:S(2)}) copy-start(bf16[1024,4608]{1,0:T(8,128)(2,1)} %get-tuple-element.85) | copy-start | bytes 28311556 | tf_op jit(solution)/shard_map/cond
  41.6 5.8 %copy-start.27 = (f32[640,2304]{1,0:T(8,128)}, f32[640,2304]{1,0:T(8,128)S(1)}, u32[]{:S(2)}) copy-start(f32[640,2304]{1,0:T(8,128)S(1)} %convolution_multiply_fusion.13) | copy-start | bytes 17694724 | tf_op jit(solution)/shard_map/cond
  41.8 2.3 %copy-start.83 = (bf16[1024,640]{1,0:T(8,128)(2,1)S(1)}, bf16[1024,640]{1,0:T(8,128)(2,1)}, u32[]{:S(2)}) copy-start(bf16[1024,640]{1,0:T(8,128)(2,1)} %get-tuple-element.84) | copy-start | bytes 3932164 | tf_op jit(solution)/shard_map/cond
  42.0 9.7 %collective-permute-start.84 = (bf16[2,160,2304]{2,1,0:T(8,128)(2,1)S(1)}, bf16[2,160,2304]{2,1,0:T(8,128)(2,1)S(1)}, u32[]{:S(2)}, u32[]{:S(2)}) collective-permute-start(bf16[2,160,2304]{2,1,0:T(8,128)(2,1)S(1)} %pad_maximum_fusion.12), channel_id=1, source_target_pairs={{0,8},{8,0},{16,24},{24,16},{1,9},{9,1},{17,25},{25,17},{2,10},{10... | collective-permute-start | bytes 4423688 | tf_op jit(solution)/shard_map/cond/branch_6_fun/ppermute | solution.py:14
  47.4 2.6 %copy-start.28 = (f32[640,2304]{1,0:T(8,128)}, f32[640,2304]{1,0:T(8,128)S(1)}, u32[]{:S(2)}) copy-start(f32[640,2304]{1,0:T(8,128)S(1)} %convolution_multiply_fusion.12) | copy-start | bytes 17694724 | tf_op jit(solution)/shard_map/cond
  51.2 7.6 %collective-permute-start.94 = (bf16[2,160,2304]{2,1,0:T(8,128)(2,1)}, bf16[2,160,2304]{2,1,0:T(8,128)(2,1)}, u32[]{:S(2)}, u32[]{:S(2)}) collective-permute-start(bf16[2,160,2304]{2,1,0:T(8,128)(2,1)} %pad_maximum_fusion.13), channel_id=1, source_target_pairs={{0,8},{8,0},{16,24},{24,16},{1,9},{9,1},{17,25},{25,17},{2,10},{10... | collective-permute-start | bytes 4423688 | tf_op jit(solution)/shard_map/cond/branch_6_fun/ppermute | solution.py:14
  51.7 4.6 %copy-start.58 = (bf16[2,160,2304]{2,1,0:T(8,128)(2,1)}, bf16[2,160,2304]{2,1,0:T(8,128)(2,1)S(1)}, u32[]{:S(2)}) copy-start(bf16[2,160,2304]{2,1,0:T(8,128)(2,1)S(1)} %collective-permute-done.84) | copy-start | bytes 4423684 | tf_op jit(solution)/shard_map/cond
  51.7 7.1 %copy-start.29 = (f32[640,2304]{1,0:T(8,128)S(1)}, f32[640,2304]{1,0:T(8,128)}, u32[]{:S(2)}) copy-start(f32[640,2304]{1,0:T(8,128)} %copy-done.28) | copy-start | bytes 17694724 | tf_op jit(solution)/shard_map/cond
  56.3 20.2 %collective-permute-start.85 = (bf16[1,160,2304]{2,1,0:T(8,128)(2,1)}, bf16[1,160,2304]{2,1,0:T(8,128)(2,1)}, u32[]{:S(2)}, u32[]{:S(2)}) collective-permute-start(bf16[1,160,2304]{2,1,0:T(8,128)(2,1)} %fusion.102), channel_id=1, source_target_pairs={{0,16},{8,24},{16,0},{24,8},{1,17},{9,25},{17,1},{25,9},{2,18},{10... | collective-permute-start | bytes 2211848 | tf_op jit(solution)/shard_map/cond/branch_6_fun/ppermute | solution.py:14
  58.8 33.3 %copy-start.6 = (f32[160,4608]{1,0:T(8,128)S(1)}, f32[160,4608]{1,0:T(8,128)}, u32[]{:S(2)}) copy-start(f32[160,4608]{1,0:T(8,128)} %get-tuple-element.82) | copy-start | bytes 8847364 | tf_op jit(solution)/shard_map/cond
  61.6 30.5 %collective-permute-start.95 = (bf16[1,160,2304]{2,1,0:T(8,128)(2,1)}, bf16[1,160,2304]{2,1,0:T(8,128)(2,1)}, u32[]{:S(2)}, u32[]{:S(2)}) collective-permute-start(bf16[1,160,2304]{2,1,0:T(8,128)(2,1)} %fusion.105), channel_id=1, source_target_pairs={{0,16},{8,24},{16,0},{24,8},{1,17},{9,25},{17,1},{25,9},{2,18},{10... | collective-permute-start | bytes 2211848 | tf_op jit(solution)/shard_map/cond/branch_6_fun/ppermute | solution.py:14
  98.8 10.5 %collective-permute-start.86 = (bf16[80,2304]{1,0:T(8,128)(2,1)S(1)}, bf16[80,2304]{1,0:T(8,128)(2,1)S(1)}, u32[]{:S(2)}, u32[]{:S(2)}) collective-permute-start(bf16[80,2304]{1,0:T(8,128)(2,1)S(1)} %select_convert_fusion.49), channel_id=1, source_target_pairs={{0,1},{1,0},{2,3},{3,2},{4,5},{5,4},{6,7},{7,6},{8,9},{9,8},{10,11... | collective-permute-start | bytes 1105928 | tf_op jit(solution)/shard_map/cond/branch_6_fun/ppermute | solution.py:14
  100.6 10.5 %collective-permute-start.96 = (bf16[80,2304]{1,0:T(8,128)(2,1)S(1)}, bf16[80,2304]{1,0:T(8,128)(2,1)S(1)}, u32[]{:S(2)}, u32[]{:S(2)}) collective-permute-start(bf16[80,2304]{1,0:T(8,128)(2,1)S(1)} %select_convert_fusion.48), channel_id=1, source_target_pairs={{0,2},{1,3},{2,0},{3,1},{4,6},{5,7},{6,4},{7,5},{8,10},{9,11},{10,... | collective-permute-start | bytes 1105928 | tf_op jit(solution)/shard_map/cond/branch_6_fun/ppermute | solution.py:14
  109.4 5.7 %collective-permute-start.87 = (bf16[40,2304]{1,0:T(8,128)(2,1)S(1)}, bf16[40,2304]{1,0:T(8,128)(2,1)S(1)}, u32[]{:S(2)}, u32[]{:S(2)}) collective-permute-start(bf16[40,2304]{1,0:T(8,128)(2,1)S(1)} %select_convert_fusion.51), channel_id=1, source_target_pairs={{0,2},{1,3},{2,0},{3,1},{4,6},{5,7},{6,4},{7,5},{8,10},{9,11},{10,... | collective-permute-start | bytes 552968 | tf_op jit(solution)/shard_map/cond/branch_6_fun/ppermute | solution.py:14
  111.2 6.5 %collective-permute-start.97 = (bf16[40,2304]{1,0:T(8,128)(2,1)S(1)}, bf16[40,2304]{1,0:T(8,128)(2,1)S(1)}, u32[]{:S(2)}, u32[]{:S(2)}) collective-permute-start(bf16[40,2304]{1,0:T(8,128)(2,1)S(1)} %select_convert_fusion.50), channel_id=1, source_target_pairs={{0,1},{1,0},{2,3},{3,2},{4,5},{5,4},{6,7},{7,6},{8,9},{9,8},{10,11... | collective-permute-start | bytes 552968 | tf_op jit(solution)/shard_map/cond/branch_6_fun/ppermute | solution.py:14
  115.2 14.5 %collective-permute-start.88 = (bf16[40,2304]{1,0:T(8,128)(2,1)S(1)}, bf16[40,2304]{1,0:T(8,128)(2,1)S(1)}, u32[]{:S(2)}, u32[]{:S(2)}) collective-permute-start(bf16[40,2304]{1,0:T(8,128)(2,1)S(1)} %get-tuple-element.158), channel_id=1, source_target_pairs={{0,4},{1,5},{2,6},{3,7},{4,0},{5,1},{6,2},{7,3},{8,12},{9,13},{10,... | collective-permute-start | bytes 552968 | tf_op jit(solution)/shard_map/cond/branch_6_fun/ppermute | solution.py:14
  117.8 14.9 %collective-permute-start.98 = (bf16[40,2304]{1,0:T(8,128)(2,1)S(1)}, bf16[40,2304]{1,0:T(8,128)(2,1)S(1)}, u32[]{:S(2)}, u32[]{:S(2)}) collective-permute-start(bf16[40,2304]{1,0:T(8,128)(2,1)S(1)} %get-tuple-element.153), channel_id=1, source_target_pairs={{0,4},{1,5},{2,6},{3,7},{4,0},{5,1},{6,2},{7,3},{8,12},{9,13},{10,... | collective-permute-start | bytes 552968 | tf_op jit(solution)/shard_map/cond/branch_6_fun/ppermute | solution.py:14
  129.7 6.9 %collective-permute-start.89 = (bf16[40,2304]{1,0:T(8,128)(2,1)S(1)}, bf16[40,2304]{1,0:T(8,128)(2,1)S(1)}, u32[]{:S(2)}, u32[]{:S(2)}) collective-permute-start(bf16[40,2304]{1,0:T(8,128)(2,1)S(1)} %fusion.108), channel_id=1, source_target_pairs={{0,2},{1,3},{2,0},{3,1},{4,6},{5,7},{6,4},{7,5},{8,10},{9,11},{10,... | collective-permute-start | bytes 552968 | tf_op jit(solution)/shard_map/cond/branch_6_fun/ppermute | solution.py:14
  132.8 5.7 %collective-permute-start.99 = (bf16[40,2304]{1,0:T(8,128)(2,1)S(1)}, bf16[40,2304]{1,0:T(8,128)(2,1)S(1)}, u32[]{:S(2)}, u32[]{:S(2)}) collective-permute-start(bf16[40,2304]{1,0:T(8,128)(2,1)S(1)} %fusion.109), channel_id=1, source_target_pairs={{0,1},{1,0},{2,3},{3,2},{4,5},{5,4},{6,7},{7,6},{8,9},{9,8},{10,11... | collective-permute-start | bytes 552968 | tf_op jit(solution)/shard_map/cond/branch_6_fun/ppermute | solution.py:14
  136.7 10.0 %collective-permute-start.90 = (bf16[80,2304]{1,0:T(8,128)(2,1)S(1)}, bf16[80,2304]{1,0:T(8,128)(2,1)S(1)}, u32[]{:S(2)}, u32[]{:S(2)}) collective-permute-start(bf16[80,2304]{1,0:T(8,128)(2,1)S(1)} %fusion.107), channel_id=1, source_target_pairs={{0,1},{1,0},{2,3},{3,2},{4,5},{5,4},{6,7},{7,6},{8,9},{9,8},{10,11... | collective-permute-start | bytes 1105928 | tf_op jit(solution)/shard_map/cond/branch_6_fun/ppermute | solution.py:14
  138.6 0.8 copy-start.69
  140.2 13.5 %collective-permute-start.100 = (bf16[80,2304]{1,0:T(8,128)(2,1)}, bf16[80,2304]{1,0:T(8,128)(2,1)}, u32[]{:S(2)}, u32[]{:S(2)}) collective-permute-start(bf16[80,2304]{1,0:T(8,128)(2,1)} %fusion.106), channel_id=1, source_target_pairs={{0,2},{1,3},{2,0},{3,1},{4,6},{5,7},{6,4},{7,5},{8,10},{9,11},{10,... | collective-permute-start | bytes 1105928 | tf_op jit(solution)/shard_map/cond/branch_6_fun/ppermute | solution.py:14
  146.8 1.8 copy-start.16
  150.5 2.6 %copy-start.48 = (bf16[1,640,4608]{2,1,0:T(8,128)(2,1)}, bf16[1,640,4608]{2,1,0:T(8,128)(2,1)S(1)}, u32[]{:S(2)}) copy-start(bf16[1,640,4608]{2,1,0:T(8,128)(2,1)S(1)} %get-tuple-element.155) | copy-start | bytes 17694724 | tf_op jit(solution)/shard_map/cond
  153.0 17.3 %collective-permute-start.91 = (bf16[160,2304]{1,0:T(8,128)(2,1)}, bf16[160,2304]{1,0:T(8,128)(2,1)}, u32[]{:S(2)}, u32[]{:S(2)}) collective-permute-start(bf16[160,2304]{1,0:T(8,128)(2,1)} %get-tuple-element.156), channel_id=1, source_target_pairs={{0,16},{8,24},{16,0},{24,8},{1,17},{9,25},{17,1},{25,9},{2,18},{10... | collective-permute-start | bytes 2211848 | tf_op jit(solution)/shard_map/cond/branch_6_fun/ppermute | solution.py:14
  153.6 18.7 %collective-permute-start.92 = (bf16[160,2304]{1,0:T(8,128)(2,1)}, bf16[160,2304]{1,0:T(8,128)(2,1)S(1)}, u32[]{:S(2)}, u32[]{:S(2)}) collective-permute-start(bf16[160,2304]{1,0:T(8,128)(2,1)} %get-tuple-element.156), channel_id=1, source_target_pairs={{0,8},{8,0},{16,24},{24,16},{1,9},{9,1},{17,25},{25,17},{2,10},{10... | collective-permute-start | bytes 2211848 | tf_op jit(solution)/shard_map/cond/branch_6_fun/ppermute | solution.py:14
  170.3 2.9 %collective-permute-start.93 = (bf16[160,2304]{1,0:T(8,128)(2,1)}, bf16[160,2304]{1,0:T(8,128)(2,1)S(1)}, u32[]{:S(2)}, u32[]{:S(2)}) collective-permute-start(bf16[160,2304]{1,0:T(8,128)(2,1)} %collective-permute-done.91), channel_id=1, source_target_pairs={{0,8},{8,0},{16,24},{24,16},{1,9},{9,1},{17,25},{25,17},{2,10},{10... | collective-permute-start | bytes 2211848 | tf_op jit(solution)/shard_map/cond/branch_6_fun/ppermute | solution.py:14
  172.4 2.4 %copy-start.17 = (f32[160,4608]{1,0:T(8,128)S(1)}, f32[160,4608]{1,0:T(8,128)}, u32[]{:S(2)}) copy-start(f32[160,4608]{1,0:T(8,128)} %get-tuple-element.83) | copy-start | bytes 8847364 | tf_op jit(solution)/shard_map/cond
  174.7 1.8 copy-start.68
  176.0 18.9 %collective-permute-start.101 = (bf16[160,2304]{1,0:T(8,128)(2,1)S(1)}, bf16[160,2304]{1,0:T(8,128)(2,1)S(1)}, u32[]{:S(2)}, u32[]{:S(2)}) collective-permute-start(bf16[160,2304]{1,0:T(8,128)(2,1)S(1)} %get-tuple-element.151), channel_id=1, source_target_pairs={{0,16},{8,24},{16,0},{24,8},{1,17},{9,25},{17,1},{25,9},{2,18},{10... | collective-permute-start | bytes 2211848 | tf_op jit(solution)/shard_map/cond/branch_6_fun/ppermute | solution.py:14
  176.3 19.5 %collective-permute-start.102 = (bf16[160,2304]{1,0:T(8,128)(2,1)S(1)}, bf16[160,2304]{1,0:T(8,128)(2,1)S(1)}, u32[]{:S(2)}, u32[]{:S(2)}) collective-permute-start(bf16[160,2304]{1,0:T(8,128)(2,1)S(1)} %get-tuple-element.151), channel_id=1, source_target_pairs={{0,8},{8,0},{16,24},{24,16},{1,9},{9,1},{17,25},{25,17},{2,10},{10... | collective-permute-start | bytes 2211848 | tf_op jit(solution)/shard_map/cond/branch_6_fun/ppermute | solution.py:14
  194.9 2.2 %collective-permute-start.103 = (bf16[160,2304]{1,0:T(8,128)(2,1)S(1)}, bf16[160,2304]{1,0:T(8,128)(2,1)S(1)}, u32[]{:S(2)}, u32[]{:S(2)}) collective-permute-start(bf16[160,2304]{1,0:T(8,128)(2,1)S(1)} %collective-permute-done.101), channel_id=1, source_target_pairs={{0,8},{8,0},{16,24},{24,16},{1,9},{9,1},{17,25},{25,17},{2,10},{10... | collective-permute-start | bytes 2211848 | tf_op jit(solution)/shard_map/cond/branch_6_fun/ppermute | solution.py:14

commit v2 on v0

v2 whole, which is shorter than its diff:
```python
import jax
import jax.numpy as jnp
from jax import lax
from jax.experimental import pallas as pl
from jax.experimental.pallas import tpu as pltpu
from jax.sharding import PartitionSpec as P

base_rate = 0.5
slow_rate = 1.0
slow_beta = 0.7
chunk_shares = (1, 1, 1, 1)


def swapped(block, axis, bit):
    count = lax.axis_size(axis)
    return lax.ppermute(block, axis, [(i, i ^ (1 << bit)) for i in range(count)])


def bit_of(index, bit):
    return jnp.bitwise_and(jnp.right_shift(index, bit), 1)


def wide(block):
    return block.astype(jnp.float32)


def narrow(block):
    return block.astype(jnp.bfloat16)


def partial_products(hidden, cotangent, bounds, scale, turned):
    node_count = lax.axis_size("node")
    tokens = cotangent.shape[0]
    height = hidden.shape[0 if turned else 1]
    rows = height // node_count
    chunk_count = len(bounds) - 1
    widest = 1280 if turned else 512
    tile = max(t for t in range(128, widest + 1, 128) if all(b % t == 0 for b in bounds))
    firsts = [(b - bounds[0]) // tile for b in bounds]

    def kernel(hidden_ref, cotangent_ref, *rest):
        core = jnp.bitwise_and(lax.axis_index("node"), 1)
        step = pl.program_id(0)
        if turned:
            left = hidden_ref
        else:
            left = rest[-1]

            @pl.when(step == 0)
            def _():
                left[...] = hidden_ref[...].T

        product = jnp.dot(left[...], cotangent_ref[...], preferred_element_type=jnp.float32)
        product = narrow(product * scale)
        for chunk in range(chunk_count):

            @pl.when((step >= firsts[chunk]) & (step < firsts[chunk + 1]))
            def _(send_ref=rest[2 * chunk], keep_ref=rest[2 * chunk + 1]):
                for pair in range(node_count // 2):
                    low = product[2 * pair * rows : (2 * pair + 1) * rows]
                    high = product[(2 * pair + 1) * rows : (2 * pair + 2) * rows]
                    send_ref[pair] = jnp.where(core == 1, low, high)
                    keep_ref[pair] = jnp.where(core == 1, high, low)

    shapes, specs = [], []
    for chunk in range(chunk_count):
        first, end = firsts[chunk], firsts[chunk + 1]
        shape = jax.ShapeDtypeStruct((node_count // 2, rows, (end - first) * tile), jnp.bfloat16)
        spec = pl.BlockSpec(
            (node_count // 2, rows, tile),
            lambda j, first=first, end=end: (0, 0, jnp.clip(j, first, end - 1) - first),
        )
        shapes += [shape, shape]
        specs += [spec, spec]
    if not turned:
        shapes.append(jax.ShapeDtypeStruct((height, tokens), jnp.bfloat16))
        specs.append(pl.BlockSpec((height, tokens), lambda j: (0, 0)))
    part = bounds[-1] - bounds[0]
    return pl.pallas_call(
        kernel,
        grid=(part // tile,),
        out_shape=shapes,
        in_specs=[
            pl.BlockSpec(hidden.shape, lambda j: (0, 0)),
            pl.BlockSpec((tokens, tile), lambda j: (0, bounds[0] // tile + j)),
        ],
        out_specs=specs,
        compiler_params=pltpu.CompilerParams(vmem_limit_bytes=32 * 2**20),
        cost_estimate=pl.CostEstimate(
            flops=2 * tokens * height * part,
            bytes_accessed=2 * (tokens * height + tokens * part + height * part),
            transcendentals=0,
        ),
    )(hidden, cotangent)


any_place = pl.BlockSpec(memory_space=pl.ANY)
in_hbm = pl.BlockSpec(memory_space=pltpu.HBM)
in_vmem = pl.BlockSpec(memory_space=pltpu.VMEM)


def small_kernel(body, ins, in_specs, outs, out_specs, scratch=(), aliases=None):
    return pl.pallas_call(
        body,
        out_shape=outs,
        in_specs=in_specs,
        out_specs=out_specs,
        scratch_shapes=list(scratch),
        input_output_aliases=aliases or {},
        compiler_params=pltpu.CompilerParams(vmem_limit_bytes=12 * 2**20),
        cost_estimate=pl.CostEstimate(flops=1024, bytes_accessed=1024, transcendentals=0),
    )(*ins)


def by_rows(count, step):
    @pl.loop(0, count // 16)
    def _(group):
        step(pl.multiple_of(group * 16, 16))


def reduced_over_cores(keep, got, anchor, start):
    rows, part = keep.shape[1:]

    def kernel(keep_ref, got_ref, anchor_ref, send_ref, base_ref, held, sem):
        mine = bit_of(lax.axis_index("node"), 1)
        copy = pltpu.make_async_copy(anchor_ref.at[:, pl.ds(start, part)], held, sem)
        copy.start()

        def for_other(row):
            group = pl.ds(row, 16)
            send_ref[group] = narrow(wide(keep_ref[1 - mine, group]) + wide(got_ref[1 - mine, group]))

        by_rows(rows, for_other)
        copy.wait()

        def for_own(row):
            group = pl.ds(row, 16)
            total = wide(keep_ref[mine, group]) + wide(got_ref[mine, group])
            base_ref[group] = held[group] - base_rate * total

        by_rows(rows, for_own)

    return small_kernel(
        kernel,
        (keep, got, anchor),
        [in_vmem, in_vmem, any_place],
        [jax.ShapeDtypeStruct((rows, part), jnp.bfloat16), jax.ShapeDtypeStruct((rows, part), jnp.float32)],
        [in_vmem, in_vmem],
        [pltpu.VMEM((rows, part), jnp.float32), pltpu.SemaphoreType.DMA],
    )


def met(block, got, factor, gain, in_half, out_half):
    rows, part = got.shape
    sent = rows if out_half is None else rows // 2

    def kernel(block_ref, got_ref, send_ref, sum_ref):
        host = lax.axis_index("hst")
        first = 0 if in_half is None else bit_of(host, in_half) * rows

        def add(row):
            group = pl.ds(row, 16)
            total = block_ref[pl.ds(pl.multiple_of(first + row, 16), 16)] + factor * wide(got_ref[group])
            total = gain * total
            sum_ref[group] = total
            if out_half is None:
                send_ref[group] = narrow(total)

        by_rows(rows, add)
        if out_half is not None:
            other = (1 - bit_of(host, out_half)) * sent

            def give(row):
                send_ref[pl.ds(row, 16)] = narrow(sum_ref[pl.ds(pl.multiple_of(other + row, 16), 16)])

            by_rows(sent, give)

    return small_kernel(
        kernel,
        (block, got),
        [in_vmem, in_vmem],
        [jax.ShapeDtypeStruct((sent, part), jnp.bfloat16), jax.ShapeDtypeStruct((rows, part), jnp.float32)],
        [in_vmem, in_vmem],
    )


def finished(block, got, gain, half, anchor, momentum, momentum_out, start):
    rows = anchor.shape[0]
    part = block.shape[1]
    columns = pl.ds(start, part)

    def kernel(block_ref, got_ref, anchor_ref, momentum_ref, *rest):
        out_ref, fresh_ref, held_anchor, held_momentum, sems = rest[-5:]
        reads = [
            pltpu.make_async_copy(anchor_ref.at[:, columns], held_anchor, sems.at[0]),
            pltpu.make_async_copy(momentum_ref.at[:, columns], held_momentum, sems.at[1]),
        ]
        for read in reads:
            read.start()
        for read in reads:
            read.wait()

        def put(group, averaged):
            old, slow = held_anchor[group], held_momentum[group]
            fresh_ref[group] = narrow(
                (1.0 - slow_rate) * old + slow_rate * averaged - slow_rate * base_rate * slow_beta * slow
            )
            held_momentum[group] = slow_beta * slow + (old - averaged) * (1.0 / base_rate)

        if half is None:
            by_rows(rows, lambda row: put(pl.ds(row, 16), gain * (block_ref[pl.ds(row, 16)] + wide(got_ref[pl.ds(row, 16)]))))
        else:
            count = rows // 2
            mine = bit_of(lax.axis_index("hst"), half) * count
            own, other = mine, count - mine
            by_rows(count, lambda row: put(pl.ds(pl.multiple_of(own + row, 16), 16), block_ref[pl.ds(row, 16)]))
            by_rows(count, lambda row: put(pl.ds(pl.multiple_of(other + row, 16), 16), wide(got_ref[pl.ds(row, 16)])))
        write = pltpu.make_async_copy(held_momentum, out_ref.at[:, columns], sems.at[0])
        write.start()
        write.wait()

    held = [] if momentum_out is None else [momentum_out]
    momentum_out, fresh = small_kernel(
        kernel,
        (block, got, anchor, momentum, *held),
        [in_vmem, in_vmem, any_place, any_place] + [in_hbm] * len(held),
        [jax.ShapeDtypeStruct(anchor.shape, jnp.float32), jax.ShapeDtypeStruct((rows, part), jnp.bfloat16)],
        [in_hbm, in_vmem],
        [pltpu.VMEM((rows, part), jnp.float32)] * 2 + [pltpu.SemaphoreType.DMA((2,))],
        {4: 0} if held else None,
    )
    return fresh, momentum_out


def placed_in(weights, shape, blocks, flips, start):
    part = blocks[0].shape[1]

    def kernel(*refs):
        out_ref, sems = refs[-2:]
        node = lax.axis_index("node")
        copies = [
            pltpu.make_async_copy(
                refs[i], out_ref.at[jnp.bitwise_xor(node, flip), :, pl.ds(start, part)], sems.at[i]
            )
            for i, flip in enumerate(flips)
        ]
        for copy in copies:
            copy.start()
        for copy in copies:
            copy.wait()

    held = [] if weights is None else [weights]
    return small_kernel(
        kernel,
        (*blocks, *held),
        [in_vmem] * len(blocks) + [in_hbm] * len(held),
        [jax.ShapeDtypeStruct(shape, jnp.bfloat16)],
        [in_hbm],
        [pltpu.SemaphoreType.DMA((len(blocks),))],
        {len(blocks): 0} if held else None,
    )[0]


def chunk_steps(plan, k, gates, base, got, start, shared):
    if got is None:
        (got,) = yield [(gates[k], "node", 1)]
    block, factor, in_half = base, -base_rate, None
    halved = []
    gain = 1.0 / (1 << len(plan))
    for place, (bit, by_halves) in enumerate(plan):
        send, block = met(block, got, factor, 1.0, in_half, bit if by_halves else None)
        (got,) = yield [(send, "hst", bit)]
        factor, in_half = 1.0, bit if by_halves else None
        halved += [bit] * by_halves
    half = None
    if halved:
        (half,) = halved
        send, block = met(block, got, factor, gain, in_half, None)
        (got,) = yield [(send, "hst", half)]
    fresh, shared["momentum"] = finished(
        block, got, gain, half, shared["anchor"], shared["momentum_in"], shared["momentum"], start
    )
    over_y, over_core = yield [(fresh, "node", 1), (fresh, "node", 0)]
    shape = shared["shape"]
    shared["weights"] = placed_in(shared["weights"], shape, [fresh, over_core, over_y], [0, 1, 2], start)
    (over_both,) = yield [(over_y, "node", 0)]
    shared["weights"] = placed_in(shared["weights"], shape, [over_both], [3], start)


def update(plan, bounds, anchor, momentum, arrived_first, *sends_and_bases):
    rows, width = anchor.shape
    node_count = lax.axis_size("node")
    shared = {
        "anchor": anchor, "momentum_in": momentum, "momentum": None, "weights": None, "shape": (node_count, rows, width),
    }
    bases, sends = list(sends_and_bases[0::2]), list(sends_and_bases[1::2])
    arrived_first, sends = lax.optimization_barrier((arrived_first, sends))
    got = [arrived_first] + [None] * (len(bases) - 1)
    gates = [None] + sends
    chunks = [
        chunk_steps(plan, k, gates, base, g, start, shared)
        for k, (base, g, start) in enumerate(zip(bases, got, bounds))
    ]
    arrived = [None] * len(chunks)
    last = None
    begun = set()
    waiting = list(range(1, len(chunks)))
    waiting = waiting[:1] + [0] + waiting[1:]
    while waiting:
        k = waiting.pop(0)
        if k in begun:
            held = {name: shared[name] for name in ("weights", "momentum") if shared[name] is not None}
            arrived[k], last, held = lax.optimization_barrier((arrived[k], last, held))
            shared.update(held)
        elif k > 1:
            gates[k], last = lax.optimization_barrier((gates[k], last))
        begun.add(k)
        try:
            moves = chunks[k].send(arrived[k])
            last = [a for a, *_ in moves]
            arrived[k] = [swapped(*move) for move in moves]
            waiting.append(k)
        except StopIteration:
            pass
    return shared["weights"].reshape(-1, width), shared["momentum"]


def plan_of(bits):
    if len(bits) < 2 or bits[-1] < 2:
        return [(b, False) for b in bits]
    return [(b, False) for b in bits[:-2]] + [(bits[-2], True), (bits[-1], False)]


def local(hidden, cotangent, anchor, momentum, round_mask):
    hidden, cotangent, anchor, momentum = hidden[0], cotangent[0], anchor[0], momentum[0]
    tokens, width = cotangent.shape
    node_count, host_count = lax.axis_size("node"), lax.axis_size("hst")
    scale = 1.0 / (tokens * node_count)
    unit = width // sum(chunk_shares)
    bounds = [unit * sum(chunk_shares[:k]) for k in range(len(chunk_shares) + 1)]
    send, keep, left = partial_products(hidden, cotangent, bounds[:2], scale, turned=False)
    send, base = reduced_over_cores(keep, swapped(send, "node", 0), anchor, 0)
    send, left = lax.optimization_barrier((send, left))
    arrived_first = swapped(send, "node", 1)
    parts = partial_products(left, cotangent, bounds[1:], scale, turned=True)
    handed = [base]
    for k in range(1, len(chunk_shares)):
        handed += reduced_over_cores(parts[2 * k - 1], swapped(parts[2 * k - 2], "node", 0), anchor, bounds[k])
    branches = []
    for mask in range(1, host_count):
        bits = [b for b in range(host_count.bit_length() - 1) if mask >> b & 1]
        branches.append(lambda *arrays, plan=plan_of(bits): update(plan, bounds, *arrays))
    weights, momentum_new = lax.switch(
        round_mask[0] - 1, branches, anchor, momentum, arrived_first, *handed
    )
    return (weights[None], momentum_new[None])


def solution(mesh):
    placed = (
        P("hst", "node", None),
        P("hst", "node", None),
        P("hst", "node", None),
        P("hst", "node", None),
        P(),
    )
    return jax.shard_map(
        local,
        mesh=mesh,
        in_specs=placed,
        out_specs=(P("hst", None, None), P("hst", "node", None)),
        check_vma=False,
    )
```

time: 275 us -> 94.1 us (0.34)
  waiting for transfers between devices: 229 us -> 40.9 us
  Pallas kernels: 0 us -> 22.7 us
  starting transfers between devices: 5.65 us -> 23.1 us
  between operations: 14.7 us -> 1.6 us
  matrix products: 10.5 us -> 0 us
  other arithmetic: 8.04 us -> 0 us
    ppermute x3 -> x24, waiting for transfers between devices: 126 us -> 40.9 us  [swapped(): return lax.ppermute(block, axis, [(i, i ^ 1 << bit) for i in range(count)])]
    reduce_scatter x1 -> x0, waiting for transfers between devices: 58.5 us -> none  [local(): lax.psum_scatter((product * token_scale).astype(jnp.bfloat16), 'node', sc...]
    all_gather x1 -> x0, waiting for transfers between devices: 44.3 us -> none  [local(): weights_whole = lax.all_gather(updated[None], 'node', axis=1, tiled=True)]
    pallas_call x0 -> x22, Pallas kernels: none -> 22.7 us  [the longest x20 12.4 us: small_kernel(): pl.pallas_call(body, out_shape=outs, in_specs=in_specs, out_specs=out_spe...]
    ppermute x3 -> x24, starting transfers between devices: 5.57 us -> 23.1 us  [swapped(): return lax.ppermute(block, axis, [(i, i ^ 1 << bit) for i in range(count)])]
    dot_general x1 -> x0, matrix products: 10.5 us -> none  [local(): lax.dot_general(tokens_here, grads_in, (((0,), (0,)), ((), ())), preferre...]
    convert_element_type x4 -> x0, other arithmetic: 8.04 us -> none  [the longest x3 4.58 us: half_step(): current.astype(jnp.bfloat16)]
    unnamed x9 -> x10, local copies, waits for them, and re-layouts: 6.9 us -> 5.01 us
  transfers between devices with their start and end apart: 5 -> 24, of which waited for: 5 -> 9; matrix products, arithmetic and copies ran while one was open for 0% -> 0% of each run, Pallas kernels for 0% -> 11%
where the time goes in v2:
time: 94.1 us; the launch traced here: 93.8 us
  waiting for transfers between devices  40.9 us (43%)
  starting transfers between devices  23.1 us (25%)
  Pallas kernels  22.7 us (24%)
  local copies, waits for them, and re-layouts  5.01 us (5%)
  between operations  1.6 us (2%)
    ppermute x24, waiting for transfers between devices, swapped(): return lax.ppermute(block, axis, [(i, i ^ 1 << bit) for i in range(count)])  40.9 us
    ppermute x24, starting transfers between devices, swapped(): return lax.ppermute(block, axis, [(i, i ^ 1 << bit) for i in range(count)])  23.1 us
    pallas_call x20, Pallas kernels, small_kernel(): pl.pallas_call(body, out_shape=outs, in_specs=in_specs, out_specs=out_spe...  12.4 us
    pallas_call x2, Pallas kernels, partial_products(): pl.pallas_call(kernel, grid=(part // tile,), out_shape=shapes, in_specs=[...  10.2 us
    unnamed x10, local copies, waits for them, and re-layouts  5.01 us
  transfers between devices with their start and end apart: 24, of which 9 were waited for; matrix products, arithmetic and copies ran while one was open for 0% of the time, Pallas kernels for 11%

profile of v2, /device:TPU:0, one launch (start us, length us, event | category | flops | bytes accessed | tf_op | source)
XLA Modules:
  0.0 93.8 jit_solution(10899526072846385424)
XLA Ops:
  0.6 3.7 %copy-done = bf16[1,1024,4608]{2,1,0:T(8,128)(2,1)S(1)} copy-done((bf16[1,1024,4608]{2,1,0:T(8,128)(2,1)S(1)}, bf16[1,1024,4608]{2,1,0:T(8,128)(2,1)}, u32[]{:S(2)}) %copy-start) | copy-done | bytes 9437208
  4.3 1.3 %copy-done.2 = bf16[1,1024,640]{2,1,0:T(8,128)(2,1)S(1)} copy-done((bf16[1,1024,640]{2,1,0:T(8,128)(2,1)S(1)}, bf16[1,1024,640]{2,1,0:T(8,128)(2,1)}, u32[]{:S(2)}) %copy-start.2) | copy-done | bytes 1310744
  5.6 3.6 %shard_map.68 = (bf16[2,160,1152]{2,1,0:T(8,128)(2,1)S(1)}, bf16[2,160,1152]{2,1,0:T(8,128)(2,1)S(1)}, bf16[640,1024]{1,0:T(8,128)(2,1)S(1)}) custom-call(bf16[1024,640]{1,0:T(8,128)(2,1)S(1)} %bitcast.15, bf16[1024,4608]{1,0:T(8,128)(2,1)S(1)} %bitcast.13), custom_call_target="tpu_custom_call" | custom-call | flops 1509949440 | bytes 5144576 | tf_op jit(solution)/shard_map/pallas_call | solution.py:79
  9.7 1.8 %collective-permute-done.165.got_ref = bf16[2,160,1152]{2,1,0:T(8,128)(2,1)S(1)} collective-permute-done((bf16[2,160,1152]{2,1,0:T(8,128)(2,1)S(1)}, bf16[2,160,1152]{2,1,0:T(8,128)(2,1)S(1)}, u32[]{:S(2)}, u32[]{:S(2)}) %collective-permute-start.165) | collective-permute-done | bytes 737312 | tf_op jit(solution)/shard_map/ppermute | solution.py:16
  11.6 1.3 %shard_map.69 = (bf16[160,1152]{1,0:T(8,128)(2,1)S(1)}, f32[160,1152]{1,0:T(8,128)S(1)}) custom-call(bf16[2,160,1152]{2,1,0:T(8,128)(2,1)S(1)} %get-tuple-element.771.keep_ref, bf16[2,160,1152]{2,1,0:T(8,128)(2,1)S(1)} %collective-permute-done.165.got_ref, f32[160,4608]{1,0:T(8,128)} %bitcast.16), custom_call_target="tpu_custom_call" | custom-call | flops 1024 | bytes 1024 | tf_op jit(solution)/shard_map/pallas_call | solution.py:103
  12.9 6.6 %shard_map.70 = (bf16[2,160,1152]{2,1,0:T(8,128)(2,1)S(1)}, bf16[2,160,1152]{2,1,0:T(8,128)(2,1)S(1)}, bf16[2,160,1152]{2,1,0:T(8,128)(2,1)S(1)}, bf16[2,160,115...) custom-call(bf16[640,1024]{1,0:T(8,128)(2,1)S(1)} %get-tuple-element.776.hidden_ref, ...), custom_call_target="tpu_custom_call" | custom-call | flops 4529848320 | bytes 12812288 | tf_op jit(solution)/shard_map/pallas_call | solution.py:79
  20.5 2.7 %collective-permute-start.166 = (bf16[160,1152]{1,0:T(8,128)(2,1)S(1)}, bf16[160,1152]{1,0:T(8,128)(2,1)S(1)}, u32[]{:S(2)}, u32[]{:S(2)}) collective-permute-start(bf16[160,1152]{1,0:T(8,128)(2,1)S(1)} %get-tuple-element.775), channel_id=1, source_target_pairs={{0,16},{8,24},{16,0},{24,8},{1,17},{9,25},{17,1},{25,9},{2,18},{10... | collective-permute-start | bytes 1105928 | tf_op jit(solution)/shard_map/ppermute | solution.py:16
  25.2 7.1 %collective-permute-done.166 = bf16[160,1152]{1,0:T(8,128)(2,1)S(1)} collective-permute-done((bf16[160,1152]{1,0:T(8,128)(2,1)S(1)}, bf16[160,1152]{1,0:T(8,128)(2,1)S(1)}, u32[]{:S(2)}, u32[]{:S(2)}) %collective-permute-start.166) | collective-permute-done | bytes 368672 | tf_op jit(solution)/shard_map/ppermute | solution.py:16
  32.3 61.3 %conditional.1 = (f32[160,4608]{1,0:T(8,128)}, bf16[1,640,4608]{2,1,0:T(8,128)(2,1)}) conditional(s32[]{:T(128)} %bitcast.7, (bf16[160,1152]{1,0:T(8,128)(2,1)S(1)}, bf16[160,1152]{1,0:T(8,128)(2,1)S(1)}, bf16[160,1152]{1,0:T(8,128)(2,1)S(1)}, bf16[160,1152]{1,0:T(8,128)(2,1)S(1)}, f32[160,1152]{1,0:T(8,128)S(1)}, ...), branch_computations={%region_0.0_spmd, %region_1.0_spmd, %region_2.0_spmd, %region_3.0_... | conditional | flops 28672 | bytes 48690436 | solution.py:353
  32.3 1.7 %collective-permute-start.22 = (bf16[160,1152]{1,0:T(8,128)(2,1)S(1)}, bf16[160,1152]{1,0:T(8,128)(2,1)S(1)}, u32[]{:S(2)}, u32[]{:S(2)}) collective-permute-start(bf16[160,1152]{1,0:T(8,128)(2,1)S(1)} %get-tuple-element.229), channel_id=1, source_target_pairs={{0,16},{8,24},{16,0},{24,8},{1,17},{9,25},{17,1},{25,9},{2,18},{10... | collective-permute-start | bytes 1105928 | tf_op jit(solution)/shard_map/cond/branch_1_fun/ppermute | solution.py:16
  34.2 1.6 %collective-permute-start.21 = (bf16[160,1152]{1,0:T(8,128)(2,1)S(1)}, bf16[160,1152]{1,0:T(8,128)(2,1)S(1)}, u32[]{:S(2)}, u32[]{:S(2)}) collective-permute-start(bf16[160,1152]{1,0:T(8,128)(2,1)S(1)} %get-tuple-element.223), channel_id=1, source_target_pairs={{0,2},{1,3},{2,0},{3,1},{4,6},{5,7},{6,4},{7,5},{8,10},{9,11},{10,... | collective-permute-start | bytes 1105928 | tf_op jit(solution)/shard_map/cond/branch_1_fun/ppermute | solution.py:16
  36.3 1.5 %collective-permute-start.19 = (bf16[160,1152]{1,0:T(8,128)(2,1)S(1)}, bf16[160,1152]{1,0:T(8,128)(2,1)S(1)}, u32[]{:S(2)}, u32[]{:S(2)}) collective-permute-start(bf16[160,1152]{1,0:T(8,128)(2,1)S(1)} %get-tuple-element.225), channel_id=1, source_target_pairs={{0,16},{8,24},{16,0},{24,8},{1,17},{9,25},{17,1},{25,9},{2,18},{10... | collective-permute-start | bytes 1105928 | tf_op jit(solution)/shard_map/cond/branch_1_fun/ppermute | solution.py:16
  37.9 5.9 %collective-permute-done.22.got_ref = bf16[160,1152]{1,0:T(8,128)(2,1)S(1)} collective-permute-done((bf16[160,1152]{1,0:T(8,128)(2,1)S(1)}, bf16[160,1152]{1,0:T(8,128)(2,1)S(1)}, u32[]{:S(2)}, u32[]{:S(2)}) %collective-permute-start.22) | collective-permute-done | bytes 368672 | tf_op jit(solution)/shard_map/cond/branch_1_fun/ppermute | solution.py:16
  43.9 1.9 %collective-permute-start.27 = (bf16[160,1152]{1,0:T(8,128)(2,1)S(1)}, bf16[160,1152]{1,0:T(8,128)(2,1)S(1)}, u32[]{:S(2)}, u32[]{:S(2)}) collective-permute-start(bf16[160,1152]{1,0:T(8,128)(2,1)S(1)} %get-tuple-element.231), channel_id=1, source_target_pairs={{0,2},{1,3},{2,0},{3,1},{4,6},{5,7},{6,4},{7,5},{8,10},{9,11},{10,... | collective-permute-start | bytes 1105928 | tf_op jit(solution)/shard_map/cond/branch_1_fun/ppermute | solution.py:16
  46.4 1.6 %collective-permute-start.25 = (bf16[160,1152]{1,0:T(8,128)(2,1)S(1)}, bf16[160,1152]{1,0:T(8,128)(2,1)S(1)}, u32[]{:S(2)}, u32[]{:S(2)}) collective-permute-start(bf16[160,1152]{1,0:T(8,128)(2,1)S(1)} %get-tuple-element.235.refs_0_), channel_id=1, source_target_pairs={{0,16},{8,24},{16,0},{24,8},{1,17},{9,25},{17,1},{25,9},{2,18},{10... | collective-permute-start | bytes 1105928 | tf_op jit(solution)/shard_map/cond/branch_1_fun/ppermute | solution.py:16
  48.0 3.7 %collective-permute-done.20.got_ref = bf16[160,1152]{1,0:T(8,128)(2,1)S(1)} collective-permute-done((bf16[160,1152]{1,0:T(8,128)(2,1)S(1)}, bf16[160,1152]{1,0:T(8,128)(2,1)S(1)}, u32[]{:S(2)}, u32[]{:S(2)}) %collective-permute-start.20) | collective-permute-done | bytes 368672 | tf_op jit(solution)/shard_map/cond/branch_1_fun/ppermute | solution.py:16
  51.8 1.9 %collective-permute-start.24 = (bf16[160,1152]{1,0:T(8,128)(2,1)S(1)}, bf16[160,1152]{1,0:T(8,128)(2,1)S(1)}, u32[]{:S(2)}, u32[]{:S(2)}) collective-permute-start(bf16[160,1152]{1,0:T(8,128)(2,1)S(1)} %get-tuple-element.238), channel_id=1, source_target_pairs={{0,2},{1,3},{2,0},{3,1},{4,6},{5,7},{6,4},{7,5},{8,10},{9,11},{10,... | collective-permute-start | bytes 1105928 | tf_op jit(solution)/shard_map/cond/branch_1_fun/ppermute | solution.py:16
  53.7 5.8 %collective-permute-done.19.got_ref = bf16[160,1152]{1,0:T(8,128)(2,1)S(1)} collective-permute-done((bf16[160,1152]{1,0:T(8,128)(2,1)S(1)}, bf16[160,1152]{1,0:T(8,128)(2,1)S(1)}, u32[]{:S(2)}, u32[]{:S(2)}) %collective-permute-start.19) | collective-permute-done | bytes 368672 | tf_op jit(solution)/shard_map/cond/branch_1_fun/ppermute | solution.py:16
  59.7 1.9 %collective-permute-start.23 = (bf16[160,1152]{1,0:T(8,128)(2,1)S(1)}, bf16[160,1152]{1,0:T(8,128)(2,1)S(1)}, u32[]{:S(2)}, u32[]{:S(2)}) collective-permute-start(bf16[160,1152]{1,0:T(8,128)(2,1)S(1)} %get-tuple-element.242), channel_id=1, source_target_pairs={{0,2},{1,3},{2,0},{3,1},{4,6},{5,7},{6,4},{7,5},{8,10},{9,11},{10,... | collective-permute-start | bytes 1105928 | tf_op jit(solution)/shard_map/cond/branch_1_fun/ppermute | solution.py:16
  62.2 1.6 %collective-permute-start.33 = (bf16[160,1152]{1,0:T(8,128)(2,1)S(1)}, bf16[160,1152]{1,0:T(8,128)(2,1)S(1)}, u32[]{:S(2)}, u32[]{:S(2)}) collective-permute-start(bf16[160,1152]{1,0:T(8,128)(2,1)S(1)} %get-tuple-element.248.refs_0_), channel_id=1, source_target_pairs={{0,16},{8,24},{16,0},{24,8},{1,17},{9,25},{17,1},{25,9},{2,18},{10... | collective-permute-start | bytes 1105928 | tf_op jit(solution)/shard_map/cond/branch_1_fun/ppermute | solution.py:16
  63.8 3.7 %collective-permute-done.25.refs_2_ = bf16[160,1152]{1,0:T(8,128)(2,1)S(1)} collective-permute-done((bf16[160,1152]{1,0:T(8,128)(2,1)S(1)}, bf16[160,1152]{1,0:T(8,128)(2,1)S(1)}, u32[]{:S(2)}, u32[]{:S(2)}) %collective-permute-start.25) | collective-permute-done | bytes 368672 | tf_op jit(solution)/shard_map/cond/branch_1_fun/ppermute | solution.py:16
  68.0 1.0 %branch_1_fun.22.refs_3_ = bf16[4,160,4608]{2,1,0:T(8,128)(2,1)} custom-call(bf16[160,1152]{1,0:T(8,128)(2,1)S(1)} %get-tuple-element.235.refs_0_, bf16[160,1152]{1,0:T(8,128)(2,1)S(1)} %collective-permute-done.26.refs_1_, bf16[160,1152]{1,0:T(8,128)(2,1)S(1)} %collective-permute-done.25.refs_2_), custom_call_target="tpu_custom_call" | custom-call | flops 1024 | bytes 1024 | tf_op jit(solution)/shard_map/cond/branch_1_fun/pallas_call | solution.py:103
  69.6 1.8 %collective-permute-start.30 = (bf16[160,1152]{1,0:T(8,128)(2,1)S(1)}, bf16[160,1152]{1,0:T(8,128)(2,1)S(1)}, u32[]{:S(2)}, u32[]{:S(2)}) collective-permute-start(bf16[160,1152]{1,0:T(8,128)(2,1)S(1)} %get-tuple-element.255.refs_0_), channel_id=1, source_target_pairs={{0,16},{8,24},{16,0},{24,8},{1,17},{9,25},{17,1},{25,9},{2,18},{10... | collective-permute-start | bytes 1105928 | tf_op jit(solution)/shard_map/cond/branch_1_fun/ppermute | solution.py:16
  72.0 3.4 %collective-permute-done.33.refs_2_ = bf16[160,1152]{1,0:T(8,128)(2,1)S(1)} collective-permute-done((bf16[160,1152]{1,0:T(8,128)(2,1)S(1)}, bf16[160,1152]{1,0:T(8,128)(2,1)S(1)}, u32[]{:S(2)}, u32[]{:S(2)}) %collective-permute-start.33) | collective-permute-done | bytes 368672 | tf_op jit(solution)/shard_map/cond/branch_1_fun/ppermute | solution.py:16
  75.4 1.8 %collective-permute-start.28 = (bf16[160,1152]{1,0:T(8,128)(2,1)S(1)}, bf16[160,1152]{1,0:T(8,128)(2,1)S(1)}, u32[]{:S(2)}, u32[]{:S(2)}) collective-permute-start(bf16[160,1152]{1,0:T(8,128)(2,1)S(1)} %get-tuple-element.260.refs_0_), channel_id=1, source_target_pairs={{0,16},{8,24},{16,0},{24,8},{1,17},{9,25},{17,1},{25,9},{2,18},{10... | collective-permute-start | bytes 1105928 | tf_op jit(solution)/shard_map/cond/branch_1_fun/ppermute | solution.py:16
  77.2 1.0 %branch_1_fun.25.refs_1_ = bf16[4,160,4608]{2,1,0:T(8,128)(2,1)} custom-call(bf16[160,1152]{1,0:T(8,128)(2,1)S(1)} %get-tuple-element.248.refs_0_, bf16[160,1152]{1,0:T(8,128)(2,1)S(1)} %collective-permute-done.34.refs_1_, bf16[160,1152]{1,0:T(8,128)(2,1)S(1)} %collective-permute-done.33.refs_2_, ...), custom_call_target="tpu_custom_call", output_to_operand_aliasing={{}: (3, {})} | custom-call | flops 1024 | bytes 1024 | tf_op jit(solution)/shard_map/cond/branch_1_fun/pallas_call | solution.py:103
  79.5 3.8 %collective-permute-done.30.refs_2_ = bf16[160,1152]{1,0:T(8,128)(2,1)S(1)} collective-permute-done((bf16[160,1152]{1,0:T(8,128)(2,1)S(1)}, bf16[160,1152]{1,0:T(8,128)(2,1)S(1)}, u32[]{:S(2)}, u32[]{:S(2)}) %collective-permute-start.30) | collective-permute-done | bytes 368672 | tf_op jit(solution)/shard_map/cond/branch_1_fun/ppermute | solution.py:16
  83.3 1.0 %branch_1_fun.27.refs_3_ = bf16[4,160,4608]{2,1,0:T(8,128)(2,1)} custom-call(bf16[160,1152]{1,0:T(8,128)(2,1)S(1)} %get-tuple-element.255.refs_0_, bf16[160,1152]{1,0:T(8,128)(2,1)S(1)} %collective-permute-done.31.refs_1_, bf16[160,1152]{1,0:T(8,128)(2,1)S(1)} %collective-permute-done.30.refs_2_, ...), custom_call_target="tpu_custom_call", output_to_operand_aliasing={{}: (3, {})} | custom-call | flops 1024 | bytes 1024 | tf_op jit(solution)/shard_map/cond/branch_1_fun/pallas_call | solution.py:103
  84.3 5.7 %collective-permute-done.28.refs_2_ = bf16[160,1152]{1,0:T(8,128)(2,1)S(1)} collective-permute-done((bf16[160,1152]{1,0:T(8,128)(2,1)S(1)}, bf16[160,1152]{1,0:T(8,128)(2,1)S(1)}, u32[]{:S(2)}, u32[]{:S(2)}) %collective-permute-start.28) | collective-permute-done | bytes 368672 | tf_op jit(solution)/shard_map/cond/branch_1_fun/ppermute | solution.py:16
  90.0 1.0 %branch_1_fun.28.refs_1_ = bf16[4,160,4608]{2,1,0:T(8,128)(2,1)} custom-call(bf16[160,1152]{1,0:T(8,128)(2,1)S(1)} %get-tuple-element.260.refs_0_, bf16[160,1152]{1,0:T(8,128)(2,1)S(1)} %collective-permute-done.29.refs_1_, bf16[160,1152]{1,0:T(8,128)(2,1)S(1)} %collective-permute-done.28.refs_2_, ...), custom_call_target="tpu_custom_call", output_to_operand_aliasing={{}: (3, {})} | custom-call | flops 1024 | bytes 1024 | tf_op jit(solution)/shard_map/cond/branch_1_fun/pallas_call | solution.py:103
  91.8 0.8 branch_1_fun.30.refs_1_
  92.6 0.8 branch_1_fun.31
  (51 shorter events, 8.7 us)
Async XLA Ops:
  0.6 3.7 %copy-start = (bf16[1,1024,4608]{2,1,0:T(8,128)(2,1)S(1)}, bf16[1,1024,4608]{2,1,0:T(8,128)(2,1)}, u32[]{:S(2)}) copy-start(bf16[1,1024,4608]{2,1,0:T(8,128)(2,1)} %param.13) | copy-start | bytes 28311556
  4.3 1.3 %copy-start.2 = (bf16[1,1024,640]{2,1,0:T(8,128)(2,1)S(1)}, bf16[1,1024,640]{2,1,0:T(8,128)(2,1)}, u32[]{:S(2)}) copy-start(bf16[1,1024,640]{2,1,0:T(8,128)(2,1)} %param.12) | copy-start | bytes 3932164
  5.6 7.3 %copy-start.1 = (bf16[1,1024,4608]{2,1,0:T(8,128)(2,1)S(1)}, bf16[1,1024,4608]{2,1,0:T(8,128)(2,1)}, u32[]{:S(2)}) copy-start(bf16[1,1024,4608]{2,1,0:T(8,128)(2,1)} %param.13) | copy-start | bytes 28311556
  9.2 2.4 %collective-permute-start.165 = (bf16[2,160,1152]{2,1,0:T(8,128)(2,1)S(1)}, bf16[2,160,1152]{2,1,0:T(8,128)(2,1)S(1)}, u32[]{:S(2)}, u32[]{:S(2)}) collective-permute-start(bf16[2,160,1152]{2,1,0:T(8,128)(2,1)S(1)} %get-tuple-element.772), channel_id=1, source_target_pairs={{0,8},{8,0},{16,24},{24,16},{1,9},{9,1},{17,25},{25,17},{2,10},{10... | collective-permute-start | bytes 2211848 | tf_op jit(solution)/shard_map/ppermute | solution.py:16
  12.9 10.9 %copy-start.3 = (f32[1,160,4608]{2,1,0:T(8,128)S(1)}, f32[1,160,4608]{2,1,0:T(8,128)}, u32[]{:S(2)}) copy-start(f32[1,160,4608]{2,1,0:T(8,128)} %param.14) | copy-start | bytes 8847364
  19.6 4.3 %collective-permute-start.169 = (bf16[2,160,1152]{2,1,0:T(8,128)(2,1)S(1)}, bf16[2,160,1152]{2,1,0:T(8,128)(2,1)S(1)}, u32[]{:S(2)}, u32[]{:S(2)}) collective-permute-start(bf16[2,160,1152]{2,1,0:T(8,128)(2,1)S(1)} %get-tuple-element.784), channel_id=1, source_target_pairs={{0,8},{8,0},{16,24},{24,16},{1,9},{9,1},{17,25},{25,17},{2,10},{10... | collective-permute-start | bytes 2211848 | tf_op jit(solution)/shard_map/ppermute | solution.py:16
  20.0 4.3 %collective-permute-start.168 = (bf16[2,160,1152]{2,1,0:T(8,128)(2,1)S(1)}, bf16[2,160,1152]{2,1,0:T(8,128)(2,1)S(1)}, u32[]{:S(2)}, u32[]{:S(2)}) collective-permute-start(bf16[2,160,1152]{2,1,0:T(8,128)(2,1)S(1)} %get-tuple-element.781), channel_id=1, source_target_pairs={{0,8},{8,0},{16,24},{24,16},{1,9},{9,1},{17,25},{25,17},{2,10},{10... | collective-permute-start | bytes 2211848 | tf_op jit(solution)/shard_map/ppermute | solution.py:16
  20.1 4.6 %collective-permute-start.167 = (bf16[2,160,1152]{2,1,0:T(8,128)(2,1)S(1)}, bf16[2,160,1152]{2,1,0:T(8,128)(2,1)S(1)}, u32[]{:S(2)}, u32[]{:S(2)}) collective-permute-start(bf16[2,160,1152]{2,1,0:T(8,128)(2,1)S(1)} %get-tuple-element.778), channel_id=1, source_target_pairs={{0,8},{8,0},{16,24},{24,16},{1,9},{9,1},{17,25},{25,17},{2,10},{10... | collective-permute-start | bytes 2211848 | tf_op jit(solution)/shard_map/ppermute | solution.py:16
  20.5 11.8 %collective-permute-start.166 = (bf16[160,1152]{1,0:T(8,128)(2,1)S(1)}, bf16[160,1152]{1,0:T(8,128)(2,1)S(1)}, u32[]{:S(2)}, u32[]{:S(2)}) collective-permute-start(bf16[160,1152]{1,0:T(8,128)(2,1)S(1)} %get-tuple-element.775), channel_id=1, source_target_pairs={{0,16},{8,24},{16,0},{24,8},{1,17},{9,25},{17,1},{25,9},{2,18},{10... | collective-permute-start | bytes 1105928 | tf_op jit(solution)/shard_map/ppermute | solution.py:16
  23.9 8.4 %copy-start.4 = (f32[1,160,4608]{2,1,0:T(8,128)S(1)}, f32[1,160,4608]{2,1,0:T(8,128)}, u32[]{:S(2)}) copy-start(f32[1,160,4608]{2,1,0:T(8,128)} %param.15) | copy-start | bytes 8847364
  32.3 11.5 %collective-permute-start.22 = (bf16[160,1152]{1,0:T(8,128)(2,1)S(1)}, bf16[160,1152]{1,0:T(8,128)(2,1)S(1)}, u32[]{:S(2)}, u32[]{:S(2)}) collective-permute-start(bf16[160,1152]{1,0:T(8,128)(2,1)S(1)} %get-tuple-element.229), channel_id=1, source_target_pairs={{0,16},{8,24},{16,0},{24,8},{1,17},{9,25},{17,1},{25,9},{2,18},{10... | collective-permute-start | bytes 1105928 | tf_op jit(solution)/shard_map/cond/branch_1_fun/ppermute | solution.py:16
  34.2 11.6 %collective-permute-start.21 = (bf16[160,1152]{1,0:T(8,128)(2,1)S(1)}, bf16[160,1152]{1,0:T(8,128)(2,1)S(1)}, u32[]{:S(2)}, u32[]{:S(2)}) collective-permute-start(bf16[160,1152]{1,0:T(8,128)(2,1)S(1)} %get-tuple-element.223), channel_id=1, source_target_pairs={{0,2},{1,3},{2,0},{3,1},{4,6},{5,7},{6,4},{7,5},{8,10},{9,11},{10,... | collective-permute-start | bytes 1105928 | tf_op jit(solution)/shard_map/cond/branch_1_fun/ppermute | solution.py:16
  35.8 15.8 %collective-permute-start.20 = (bf16[160,1152]{1,0:T(8,128)(2,1)S(1)}, bf16[160,1152]{1,0:T(8,128)(2,1)S(1)}, u32[]{:S(2)}, u32[]{:S(2)}) collective-permute-start(bf16[160,1152]{1,0:T(8,128)(2,1)S(1)} %get-tuple-element.224), channel_id=1, source_target_pairs={{0,16},{8,24},{16,0},{24,8},{1,17},{9,25},{17,1},{25,9},{2,18},{10... | collective-permute-start | bytes 1105928 | tf_op jit(solution)/shard_map/cond/branch_1_fun/ppermute | solution.py:16
  36.3 23.2 %collective-permute-start.19 = (bf16[160,1152]{1,0:T(8,128)(2,1)S(1)}, bf16[160,1152]{1,0:T(8,128)(2,1)S(1)}, u32[]{:S(2)}, u32[]{:S(2)}) collective-permute-start(bf16[160,1152]{1,0:T(8,128)(2,1)S(1)} %get-tuple-element.225), channel_id=1, source_target_pairs={{0,16},{8,24},{16,0},{24,8},{1,17},{9,25},{17,1},{25,9},{2,18},{10... | collective-permute-start | bytes 1105928 | tf_op jit(solution)/shard_map/cond/branch_1_fun/ppermute | solution.py:16
  43.9 17.7 %collective-permute-start.27 = (bf16[160,1152]{1,0:T(8,128)(2,1)S(1)}, bf16[160,1152]{1,0:T(8,128)(2,1)S(1)}, u32[]{:S(2)}, u32[]{:S(2)}) collective-permute-start(bf16[160,1152]{1,0:T(8,128)(2,1)S(1)} %get-tuple-element.231), channel_id=1, source_target_pairs={{0,2},{1,3},{2,0},{3,1},{4,6},{5,7},{6,4},{7,5},{8,10},{9,11},{10,... | collective-permute-start | bytes 1105928 | tf_op jit(solution)/shard_map/cond/branch_1_fun/ppermute | solution.py:16
  46.4 21.1 %collective-permute-start.25 = (bf16[160,1152]{1,0:T(8,128)(2,1)S(1)}, bf16[160,1152]{1,0:T(8,128)(2,1)S(1)}, u32[]{:S(2)}, u32[]{:S(2)}) collective-permute-start(bf16[160,1152]{1,0:T(8,128)(2,1)S(1)} %get-tuple-element.235.refs_0_), channel_id=1, source_target_pairs={{0,16},{8,24},{16,0},{24,8},{1,17},{9,25},{17,1},{25,9},{2,18},{10... | collective-permute-start | bytes 1105928 | tf_op jit(solution)/shard_map/cond/branch_1_fun/ppermute | solution.py:16
  48.0 19.5 %collective-permute-start.26 = (bf16[160,1152]{1,0:T(8,128)(2,1)S(1)}, bf16[160,1152]{1,0:T(8,128)(2,1)S(1)}, u32[]{:S(2)}, u32[]{:S(2)}) collective-permute-start(bf16[160,1152]{1,0:T(8,128)(2,1)S(1)} %get-tuple-element.235.refs_0_), channel_id=1, source_target_pairs={{0,8},{8,0},{16,24},{24,16},{1,9},{9,1},{17,25},{25,17},{2,10},{10... | collective-permute-start | bytes 1105928 | tf_op jit(solution)/shard_map/cond/branch_1_fun/ppermute | solution.py:16
  51.8 17.2 %collective-permute-start.24 = (bf16[160,1152]{1,0:T(8,128)(2,1)S(1)}, bf16[160,1152]{1,0:T(8,128)(2,1)S(1)}, u32[]{:S(2)}, u32[]{:S(2)}) collective-permute-start(bf16[160,1152]{1,0:T(8,128)(2,1)S(1)} %get-tuple-element.238), channel_id=1, source_target_pairs={{0,2},{1,3},{2,0},{3,1},{4,6},{5,7},{6,4},{7,5},{8,10},{9,11},{10,... | collective-permute-start | bytes 1105928 | tf_op jit(solution)/shard_map/cond/branch_1_fun/ppermute | solution.py:16
  59.7 11.7 %collective-permute-start.23 = (bf16[160,1152]{1,0:T(8,128)(2,1)S(1)}, bf16[160,1152]{1,0:T(8,128)(2,1)S(1)}, u32[]{:S(2)}, u32[]{:S(2)}) collective-permute-start(bf16[160,1152]{1,0:T(8,128)(2,1)S(1)} %get-tuple-element.242), channel_id=1, source_target_pairs={{0,2},{1,3},{2,0},{3,1},{4,6},{5,7},{6,4},{7,5},{8,10},{9,11},{10,... | collective-permute-start | bytes 1105928 | tf_op jit(solution)/shard_map/cond/branch_1_fun/ppermute | solution.py:16
  62.2 13.2 %collective-permute-start.33 = (bf16[160,1152]{1,0:T(8,128)(2,1)S(1)}, bf16[160,1152]{1,0:T(8,128)(2,1)S(1)}, u32[]{:S(2)}, u32[]{:S(2)}) collective-permute-start(bf16[160,1152]{1,0:T(8,128)(2,1)S(1)} %get-tuple-element.248.refs_0_), channel_id=1, source_target_pairs={{0,16},{8,24},{16,0},{24,8},{1,17},{9,25},{17,1},{25,9},{2,18},{10... | collective-permute-start | bytes 1105928 | tf_op jit(solution)/shard_map/cond/branch_1_fun/ppermute | solution.py:16
  67.5 9.7 %collective-permute-start.34 = (bf16[160,1152]{1,0:T(8,128)(2,1)S(1)}, bf16[160,1152]{1,0:T(8,128)(2,1)S(1)}, u32[]{:S(2)}, u32[]{:S(2)}) collective-permute-start(bf16[160,1152]{1,0:T(8,128)(2,1)S(1)} %get-tuple-element.248.refs_0_), channel_id=1, source_target_pairs={{0,8},{8,0},{16,24},{24,16},{1,9},{9,1},{17,25},{25,17},{2,10},{10... | collective-permute-start | bytes 1105928 | tf_op jit(solution)/shard_map/cond/branch_1_fun/ppermute | solution.py:16
  67.5 10.7 %collective-permute-start.32 = (bf16[160,1152]{1,0:T(8,128)(2,1)S(1)}, bf16[160,1152]{1,0:T(8,128)(2,1)S(1)}, u32[]{:S(2)}, u32[]{:S(2)}) collective-permute-start(bf16[160,1152]{1,0:T(8,128)(2,1)S(1)} %collective-permute-done.25.refs_2_), channel_id=1, source_target_pairs={{0,8},{8,0},{16,24},{24,16},{1,9},{9,1},{17,25},{25,17},{2,10},{10... | collective-permute-start | bytes 1105928 | tf_op jit(solution)/shard_map/cond/branch_1_fun/ppermute | solution.py:16
  69.6 13.7 %collective-permute-start.30 = (bf16[160,1152]{1,0:T(8,128)(2,1)S(1)}, bf16[160,1152]{1,0:T(8,128)(2,1)S(1)}, u32[]{:S(2)}, u32[]{:S(2)}) collective-permute-start(bf16[160,1152]{1,0:T(8,128)(2,1)S(1)} %get-tuple-element.255.refs_0_), channel_id=1, source_target_pairs={{0,16},{8,24},{16,0},{24,8},{1,17},{9,25},{17,1},{25,9},{2,18},{10... | collective-permute-start | bytes 1105928 | tf_op jit(solution)/shard_map/cond/branch_1_fun/ppermute | solution.py:16
  71.4 11.8 %collective-permute-start.31 = (bf16[160,1152]{1,0:T(8,128)(2,1)S(1)}, bf16[160,1152]{1,0:T(8,128)(2,1)S(1)}, u32[]{:S(2)}, u32[]{:S(2)}) collective-permute-start(bf16[160,1152]{1,0:T(8,128)(2,1)S(1)} %get-tuple-element.255.refs_0_), channel_id=1, source_target_pairs={{0,8},{8,0},{16,24},{24,16},{1,9},{9,1},{17,25},{25,17},{2,10},{10... | collective-permute-start | bytes 1105928 | tf_op jit(solution)/shard_map/cond/branch_1_fun/ppermute | solution.py:16
  72.0 12.3 %copy-start.6 = (f32[160,4608]{1,0:T(8,128)}, f32[160,4608]{1,0:T(8,128)S(1)}, u32[]{:S(2)}) copy-start(f32[160,4608]{1,0:T(8,128)S(1)} %get-tuple-element.794) | copy-start | bytes 8847364 | tf_op jit(solution)/shard_map/cond
  75.4 14.6 %collective-permute-start.28 = (bf16[160,1152]{1,0:T(8,128)(2,1)S(1)}, bf16[160,1152]{1,0:T(8,128)(2,1)S(1)}, u32[]{:S(2)}, u32[]{:S(2)}) collective-permute-start(bf16[160,1152]{1,0:T(8,128)(2,1)S(1)} %get-tuple-element.260.refs_0_), channel_id=1, source_target_pairs={{0,16},{8,24},{16,0},{24,8},{1,17},{9,25},{17,1},{25,9},{2,18},{10... | collective-permute-start | bytes 1105928 | tf_op jit(solution)/shard_map/cond/branch_1_fun/ppermute | solution.py:16
  77.2 12.8 %collective-permute-start.29 = (bf16[160,1152]{1,0:T(8,128)(2,1)S(1)}, bf16[160,1152]{1,0:T(8,128)(2,1)S(1)}, u32[]{:S(2)}, u32[]{:S(2)}) collective-permute-start(bf16[160,1152]{1,0:T(8,128)(2,1)S(1)} %get-tuple-element.260.refs_0_), channel_id=1, source_target_pairs={{0,8},{8,0},{16,24},{24,16},{1,9},{9,1},{17,25},{25,17},{2,10},{10... | collective-permute-start | bytes 1105928 | tf_op jit(solution)/shard_map/cond/branch_1_fun/ppermute | solution.py:16
  78.2 12.8 %collective-permute-start.37 = (bf16[160,1152]{1,0:T(8,128)(2,1)S(1)}, bf16[160,1152]{1,0:T(8,128)(2,1)S(1)}, u32[]{:S(2)}, u32[]{:S(2)}) collective-permute-start(bf16[160,1152]{1,0:T(8,128)(2,1)S(1)} %collective-permute-done.33.refs_2_), channel_id=1, source_target_pairs={{0,8},{8,0},{16,24},{24,16},{1,9},{9,1},{17,25},{25,17},{2,10},{10... | collective-permute-start | bytes 1105928 | tf_op jit(solution)/shard_map/cond/branch_1_fun/ppermute | solution.py:16
  83.3 8.5 %collective-permute-start.36 = (bf16[160,1152]{1,0:T(8,128)(2,1)S(1)}, bf16[160,1152]{1,0:T(8,128)(2,1)S(1)}, u32[]{:S(2)}, u32[]{:S(2)}) collective-permute-start(bf16[160,1152]{1,0:T(8,128)(2,1)S(1)} %collective-permute-done.30.refs_2_), channel_id=1, source_target_pairs={{0,8},{8,0},{16,24},{24,16},{1,9},{9,1},{17,25},{25,17},{2,10},{10... | collective-permute-start | bytes 1105928 | tf_op jit(solution)/shard_map/cond/branch_1_fun/ppermute | solution.py:16
  90.0 2.6 %collective-permute-start.35 = (bf16[160,1152]{1,0:T(8,128)(2,1)S(1)}, bf16[160,1152]{1,0:T(8,128)(2,1)S(1)}, u32[]{:S(2)}, u32[]{:S(2)}) collective-permute-start(bf16[160,1152]{1,0:T(8,128)(2,1)S(1)} %collective-permute-done.28.refs_2_), channel_id=1, source_target_pairs={{0,8},{8,0},{16,24},{24,16},{1,9},{9,1},{17,25},{25,17},{2,10},{10... | collective-permute-start | bytes 1105928 | tf_op jit(solution)/shard_map/cond/branch_1_fun/ppermute | solution.py:16
